TPU v7x, 256 devices: a whole 4x4x8 slice. The times are simulated.
256 devices in a mesh: blk: 8 (over y, x_hi), head: 32 (over x_lo, z, core).
Axes of the slice: x: 4 (x_hi: 2, x_lo: 2; x = x_hi * 2 + x_lo), y: 4, z: 8, core: 2. Of those that a mesh axis runs over, the one named last changes fastest.
Arguments:
- queries: bfloat16 [32768, 3072], P(('blk', 'head')), may hold values from -150 to 150
- keys_in: bfloat16 [32768, 3072], P(('blk', 'head')), may hold values from -6 to 6
- values: bfloat16 [32768, 3072], P(('blk', 'head')), may hold values from -6 to 6
- out_grad: bfloat16 [32768, 3072], P(('blk', 'head')), may hold values from -6 to 6
- doc_lengths: int32 [32], replicated, may hold values from 1 to 2048, 32768 in all
Outputs:
- query_grad: bfloat16 [32768, 3072], P(('blk', 'head'))
- key_grad: bfloat16 [32768, 3072], P(('blk', 'head'))
- value_grad: bfloat16 [32768, 3072], P(('blk', 'head'))
Inputs may be any that keep to these rules, and one draw needn't show every extreme that they name: `doc_lengths`: 32 lengths that sum to 32768; the largest is exactly 2048.
All inputs are finite; a program needn't handle non-finite values.
Results may differ from a plain program's by a relative error of at most 0.0053.
Values may be sent and summed in bfloat16 or wider, within the bound.
No kernel may reach another device: no remote copies, remote signals or barrier semaphores. Data moves between devices by JAX's collectives and lax.ppermute only.
A program may use at most 64 MiB of HBM per device.

v0:
```python
import math

import jax
import jax.numpy as jnp
from jax import lax
from jax.sharding import PartitionSpec as P

HD = 96
QBLK = 512


def from_behind(block, axis, distance):
    devices = range(lax.axis_size(axis))
    route = [(i - distance, i) for i in devices if i - distance in devices]
    return lax.ppermute(block, axis, route)


def doc_ids(doc_lengths, positions):
    starts = jnp.cumsum(doc_lengths) - doc_lengths
    return jnp.sum((starts[None, :] <= positions[:, None]).astype(jnp.int32), axis=1) - 1


def block_grads(query_blk, key_win, value_win, grad_blk, allowed, factor):
    scores = jnp.dot(query_blk, key_win.T, preferred_element_type=jnp.float32) * factor
    scores = jnp.where(allowed, scores, -1e30)
    row_max = jnp.max(scores, axis=1, keepdims=True)
    powers = jnp.exp(scores - row_max)
    shares = powers / jnp.sum(powers, axis=1, keepdims=True)
    weights = shares.astype(jnp.bfloat16)
    attended = jnp.dot(weights, value_win, preferred_element_type=jnp.float32).astype(jnp.bfloat16)
    attended = lax.optimization_barrier(attended)
    row_delta = jnp.sum(
        grad_blk.astype(jnp.float32) * attended.astype(jnp.float32), axis=1, keepdims=True
    )
    grad_value = jnp.dot(weights.T, grad_blk, preferred_element_type=jnp.float32)
    grad_prob = jnp.dot(grad_blk, value_win.T, preferred_element_type=jnp.float32)
    grad_score = (shares * (grad_prob - row_delta)).astype(jnp.bfloat16)
    grad_query = jnp.dot(grad_score, key_win, preferred_element_type=jnp.float32) * factor
    grad_key = jnp.dot(grad_score.T, query_blk, preferred_element_type=jnp.float32) * factor
    return (grad_query, grad_key, grad_value)


def sweep(query_head, grad_head, key_ext, value_ext, owners, factor, reach):
    total = query_head.shape[0]
    width = reach + QBLK

    def step(carry, block_index):
        key_acc, value_acc = carry
        start = block_index * QBLK
        query_blk = lax.dynamic_slice_in_dim(query_head, start, QBLK, 0)
        grad_blk = lax.dynamic_slice_in_dim(grad_head, start, QBLK, 0)
        key_win = lax.dynamic_slice_in_dim(key_ext, start, width, 0)
        value_win = lax.dynamic_slice_in_dim(value_ext, start, width, 0)
        owner_query = lax.dynamic_slice_in_dim(owners, start + reach, QBLK, 0)
        owner_key = lax.dynamic_slice_in_dim(owners, start, width, 0)
        causal = (
            jnp.arange(width, dtype=jnp.int32)[None, :]
            <= jnp.arange(QBLK, dtype=jnp.int32)[:, None] + reach
        )
        allowed = (owner_query[:, None] == owner_key[None, :]) & causal
        grad_query, grad_key, grad_value = block_grads(
            query_blk, key_win, value_win, grad_blk, allowed, factor
        )
        key_acc = lax.dynamic_update_slice_in_dim(
            key_acc, lax.dynamic_slice_in_dim(key_acc, start, width, 0) + grad_key, start, 0
        )
        value_acc = lax.dynamic_update_slice_in_dim(
            value_acc, lax.dynamic_slice_in_dim(value_acc, start, width, 0) + grad_value, start, 0
        )
        return ((key_acc, value_acc), grad_query.astype(jnp.bfloat16))

    zeros = jnp.zeros(key_ext.shape, jnp.float32)
    blocks = jnp.arange(total // QBLK, dtype=jnp.int32)
    (key_acc, value_acc), query_parts = lax.scan(step, (zeros, zeros), blocks)
    return (query_parts.reshape(total, query_head.shape[1]), key_acc, value_acc)


def previous_rows(key_loc, value_loc, reach):
    earlier = from_behind(jnp.stack((key_loc, value_loc)), "blk", 1)
    return (earlier[0, -reach:], earlier[1, -reach:])


def shards(queries, keys_in, values, out_grad, doc_lengths):
    factor = 1.0 / math.sqrt(HD)
    query_loc, key_loc, value_loc, grad_loc = (
        lax.all_to_all(queries, "head", split_axis=1, concat_axis=0, tiled=True),
        lax.all_to_all(keys_in, "head", split_axis=1, concat_axis=0, tiled=True),
        lax.all_to_all(values, "head", split_axis=1, concat_axis=0, tiled=True),
        lax.all_to_all(out_grad, "head", split_axis=1, concat_axis=0, tiled=True),
    )
    reach = key_loc.shape[0] // 2
    key_tail, value_tail = previous_rows(key_loc, value_loc, reach)
    span_rows = key_loc.shape[0]
    columns = key_loc.shape[1]
    heads_dev = columns // HD
    positions = (
        lax.axis_index("blk") * span_rows - reach + jnp.arange(reach + span_rows, dtype=jnp.int32)
    )
    owners = doc_ids(doc_lengths, positions)
    key_ext = jnp.concatenate([key_tail, key_loc], axis=0)
    value_ext = jnp.concatenate([value_tail, value_loc], axis=0)

    def split_heads(array):
        return array.reshape(array.shape[0], heads_dev, HD).transpose(1, 0, 2)

    def join_heads(array):
        return array.transpose(1, 0, 2).reshape(array.shape[1], columns)

    def per_head(stacked):
        return sweep(stacked[0], stacked[1], stacked[2], stacked[3], owners, factor, reach)

    grad_query, key_acc, value_acc = lax.map(
        per_head,
        (
            split_heads(query_loc),
            split_heads(grad_loc),
            split_heads(key_ext),
            split_heads(value_ext),
        ),
    )
    returned = from_behind(jnp.stack((key_acc[:, :reach], value_acc[:, :reach])), "blk", -1)
    key_own = key_acc[:, reach:].at[:, span_rows - reach :].add(returned[0])
    value_own = value_acc[:, reach:].at[:, span_rows - reach :].add(returned[1])
    query_out = join_heads(grad_query)
    key_out = join_heads(key_own.astype(jnp.bfloat16))
    value_out = join_heads(value_own.astype(jnp.bfloat16))
    return (
        lax.all_to_all(query_out, "head", split_axis=0, concat_axis=1, tiled=True),
        lax.all_to_all(key_out, "head", split_axis=0, concat_axis=1, tiled=True),
        lax.all_to_all(value_out, "head", split_axis=0, concat_axis=1, tiled=True),
    )


def solution(mesh):
    in_specs = (
        P(("blk", "head"), None),
        P(("blk", "head"), None),
        P(("blk", "head"), None),
        P(("blk", "head"), None),
        P(),
    )
    out_specs = (P(("blk", "head"), None), P(("blk", "head"), None), P(("blk", "head"), None))
    return jax.shard_map(shards, mesh=mesh, in_specs=in_specs, out_specs=out_specs, check_vma=False)
```

profile of v0, /device:TPU:17, one launch (start us, length us, event | category | flops | bytes accessed | tf_op | source)
XLA Modules:
  0.0 391.0 jit_solution(10611414537745305527)
XLA Ops:
  3.0 10.4 %all-to-all-start.1 = ((bf16[128,32,96]{0,2,1:T(8,128)(2,1)}), bf16[128,32,96]{0,2,1:T(8,128)(2,1)S(1)}, u32[]{:S(2)}, u32[]{:S(2)}) async-start(bf16[128,32,96]{0,2,1:T(8,128)(2,1)} %bitcast.6), calls=%async_computation.1 | async-start | bytes 1572864 | tf_op jit(solution)/shard_map/all_to_all | solution.py:87
  14.5 20.1 %all-to-all-done.1 = bf16[128,32,96]{0,2,1:T(8,128)(2,1)S(1)} async-done(((bf16[128,32,96]{0,2,1:T(8,128)(2,1)}), bf16[128,32,96]{0,2,1:T(8,128)(2,1)S(1)}, u32[]{:S(2)}, u32[]{:S(2)}) %all-to-all-start.1) | async-done | bytes 786464 | tf_op jit(solution)/shard_map/all_to_all | solution.py:87
  34.6 6.0 %all-to-all-start.2 = ((bf16[128,32,96]{0,2,1:T(8,128)(2,1)}), bf16[128,32,96]{0,2,1:T(8,128)(2,1)S(1)}, u32[]{:S(2)}, u32[]{:S(2)}) async-start(bf16[128,32,96]{0,2,1:T(8,128)(2,1)} %bitcast.8), calls=%async_computation.2 | async-start | bytes 1572864 | tf_op jit(solution)/shard_map/all_to_all | solution.py:88
  41.8 20.2 %all-to-all-done.2 = bf16[128,32,96]{0,2,1:T(8,128)(2,1)S(1)} async-done(((bf16[128,32,96]{0,2,1:T(8,128)(2,1)}), bf16[128,32,96]{0,2,1:T(8,128)(2,1)S(1)}, u32[]{:S(2)}, u32[]{:S(2)}) %all-to-all-start.2) | async-done | bytes 786464 | tf_op jit(solution)/shard_map/all_to_all | solution.py:88
  62.0 5.8 %all-to-all-start = ((bf16[128,32,96]{0,2,1:T(8,128)(2,1)}), bf16[128,32,96]{0,2,1:T(8,128)(2,1)S(1)}, u32[]{:S(2)}, u32[]{:S(2)}) async-start(bf16[128,32,96]{0,2,1:T(8,128)(2,1)} %bitcast.3), calls=%async_computation | async-start | bytes 1572864 | tf_op jit(solution)/shard_map/all_to_all | solution.py:86
  75.8 4.3 %collective-permute-start = (bf16[2,4096,96]{1,2,0:T(8,128)(2,1)}, bf16[2,4096,96]{1,2,0:T(8,128)(2,1)}, u32[]{:S(2)}, u32[]{:S(2)}) collective-permute-start(bf16[2,4096,96]{1,2,0:T(8,128)(2,1)} %pad_maximum_fusion), channel_id=1, source_target_pairs={{0,32},{32,64},{64,96},{96,128},{128,160},{160,192},{192,224},{1,3... | collective-permute-start | bytes 4718600 | tf_op jit(solution)/shard_map/ppermute | solution.py:15
  80.2 9.1 %all-to-all-done = bf16[128,32,96]{0,2,1:T(8,128)(2,1)S(1)} async-done(((bf16[128,32,96]{0,2,1:T(8,128)(2,1)}), bf16[128,32,96]{0,2,1:T(8,128)(2,1)S(1)}, u32[]{:S(2)}, u32[]{:S(2)}) %all-to-all-start) | async-done | bytes 786464 | tf_op jit(solution)/shard_map/all_to_all | solution.py:86
  89.2 5.8 %all-to-all-start.3 = ((bf16[128,32,96]{0,2,1:T(8,128)(2,1)}), bf16[128,32,96]{0,2,1:T(8,128)(2,1)S(1)}, u32[]{:S(2)}, u32[]{:S(2)}) async-start(bf16[128,32,96]{0,2,1:T(8,128)(2,1)} %bitcast.11), calls=%async_computation.3 | async-start | bytes 1572864 | tf_op jit(solution)/shard_map/all_to_all | solution.py:89
  96.5 30.7 %all-to-all-done.3 = bf16[128,32,96]{0,2,1:T(8,128)(2,1)S(1)} async-done(((bf16[128,32,96]{0,2,1:T(8,128)(2,1)}), bf16[128,32,96]{0,2,1:T(8,128)(2,1)S(1)}, u32[]{:S(2)}, u32[]{:S(2)}) %all-to-all-start.3) | async-done | bytes 786464 | tf_op jit(solution)/shard_map/all_to_all | solution.py:89
  132.5 147.7 %while.29 = (s32[]{:T(128)}, f32[6144,96]{0,1:T(8,128)S(1)}, f32[6144,96]{0,1:T(8,128)}, bf16[8,512,96]{1,2,0:T(8,128)(2,1)}, s32[8]{0:T(128)S(1)}, /*index=5*/s...) while((s32[]{:T(128)}, f32[6144,96]{0,1:T(8,128)S(1)}, ...), condition=%wide.region_6.7_spmd, body=%wide.region_2.6_spmd.sunk | while | flops 1530690560 | bytes 51370832 | solution.py:74
  135.3 2.7 fusion.66
  148.0 2.9 fusion.71
  153.7 2.7 fusion.66
  166.5 2.9 fusion.71
  172.2 2.7 fusion.66
  185.0 2.9 fusion.71
  203.5 2.9 fusion.71
  209.2 2.7 fusion.66
  222.0 2.9 fusion.71
  227.7 2.7 fusion.66
  240.4 2.9 fusion.71
  246.1 2.7 fusion.66
  258.9 2.9 fusion.71
  264.6 2.7 fusion.66
  277.3 2.9 fusion.71
  282.7 3.9 %collective-permute-start.1 = (f32[2,1,2048,96]{2,3,1,0:T(8,128)}, f32[2,1,2048,96]{2,3,1,0:T(8,128)}, u32[]{:S(2)}, u32[]{:S(2)}) collective-permute-start(f32[2,1,2048,96]{2,3,1,0:T(8,128)} %pad_maximum_fusion.1), channel_id=1, source_target_pairs={{32,0},{64,32},{96,64},{128,96},{160,128},{192,160},{224,192},{33,... | collective-permute-start | bytes 4718600 | tf_op jit(solution)/shard_map/ppermute | solution.py:15
  290.8 7.5 %all-to-all-start.4 = ((bf16[32,128,96]{1,2,0:T(8,128)(2,1)}), bf16[32,128,96]{1,2,0:T(8,128)(2,1)S(1)}, u32[]{:S(2)}, u32[]{:S(2)}) async-start(bf16[32,128,96]{1,2,0:T(8,128)(2,1)} %copy.82), calls=%async_computation.4 | async-start | bytes 1572864 | tf_op jit(solution)/shard_map/all_to_all | solution.py:128
  299.8 29.4 %collective-permute-done.1 = f32[2,1,2048,96]{2,3,1,0:T(8,128)} collective-permute-done((f32[2,1,2048,96]{2,3,1,0:T(8,128)}, f32[2,1,2048,96]{2,3,1,0:T(8,128)}, u32[]{:S(2)}, u32[]{:S(2)}) %collective-permute-start.1) | collective-permute-done | bytes 1572896 | tf_op jit(solution)/shard_map/ppermute | solution.py:15
  333.0 8.2 %all-to-all-start.5 = ((bf16[32,128,96]{1,2,0:T(8,128)(2,1)}), bf16[32,128,96]{1,2,0:T(8,128)(2,1)S(1)}, u32[]{:S(2)}, u32[]{:S(2)}) async-start(bf16[32,128,96]{1,2,0:T(8,128)(2,1)} %copy.83), calls=%async_computation.5 | async-start | bytes 1572864 | tf_op jit(solution)/shard_map/all_to_all | solution.py:129
  343.8 18.8 %all-to-all-done.5 = bf16[32,128,96]{1,2,0:T(8,128)(2,1)S(1)} async-done(((bf16[32,128,96]{1,2,0:T(8,128)(2,1)}), bf16[32,128,96]{1,2,0:T(8,128)(2,1)S(1)}, u32[]{:S(2)}, u32[]{:S(2)}) %all-to-all-start.5) | async-done | bytes 786464 | tf_op jit(solution)/shard_map/all_to_all | solution.py:129
  362.5 5.9 %all-to-all-start.6 = ((bf16[32,128,96]{1,2,0:T(8,128)(2,1)}), bf16[32,128,96]{1,2,0:T(8,128)(2,1)S(1)}, u32[]{:S(2)}, u32[]{:S(2)}) async-start(bf16[32,128,96]{1,2,0:T(8,128)(2,1)} %copy.84), calls=%async_computation.6 | async-start | bytes 1572864 | tf_op jit(solution)/shard_map/all_to_all | solution.py:130
  370.7 19.1 %all-to-all-done.6 = bf16[32,128,96]{1,2,0:T(8,128)(2,1)S(1)} async-done(((bf16[32,128,96]{1,2,0:T(8,128)(2,1)}), bf16[32,128,96]{1,2,0:T(8,128)(2,1)S(1)}, u32[]{:S(2)}, u32[]{:S(2)}) %all-to-all-start.6) | async-done | bytes 786464 | tf_op jit(solution)/shard_map/all_to_all | solution.py:130
  (145 shorter events, 137.0 us)
Async XLA Ops:
  0.6 12.7 %copy-start.1 = (bf16[128,3072]{1,0:T(8,128)(2,1)S(1)}, bf16[128,3072]{1,0:T(8,128)(2,1)}, u32[]{:S(2)}) copy-start(bf16[128,3072]{1,0:T(8,128)(2,1)} %param.13) | copy-start | bytes 2359300
  3.0 37.6 %copy-start.2 = (bf16[128,3072]{1,0:T(8,128)(2,1)S(1)}, bf16[128,3072]{1,0:T(8,128)(2,1)}, u32[]{:S(2)}) copy-start(bf16[128,3072]{1,0:T(8,128)(2,1)} %param.11) | copy-start | bytes 2359300
  3.0 31.6 %all-to-all-start.1 = ((bf16[128,32,96]{0,2,1:T(8,128)(2,1)}), bf16[128,32,96]{0,2,1:T(8,128)(2,1)S(1)}, u32[]{:S(2)}, u32[]{:S(2)}) async-start(bf16[128,32,96]{0,2,1:T(8,128)(2,1)} %bitcast.6), calls=%async_computation.1 | async-start | bytes 1572864 | tf_op jit(solution)/shard_map/all_to_all | solution.py:87
  34.6 33.3 %copy-start.3 = (bf16[128,3072]{1,0:T(8,128)(2,1)S(1)}, bf16[128,3072]{1,0:T(8,128)(2,1)}, u32[]{:S(2)}) copy-start(bf16[128,3072]{1,0:T(8,128)(2,1)} %param.14) | copy-start | bytes 2359300
  34.6 27.4 %all-to-all-start.2 = ((bf16[128,32,96]{0,2,1:T(8,128)(2,1)}), bf16[128,32,96]{0,2,1:T(8,128)(2,1)S(1)}, u32[]{:S(2)}, u32[]{:S(2)}) async-start(bf16[128,32,96]{0,2,1:T(8,128)(2,1)} %bitcast.8), calls=%async_computation.2 | async-start | bytes 1572864 | tf_op jit(solution)/shard_map/all_to_all | solution.py:88
  40.6 28.4 %copy-start.5 = (s32[32]{0:T(128)S(1)}, s32[32]{0:T(128)}, u32[]{:S(2)}) copy-start(s32[32]{0:T(128)} %param.15) | copy-start | bytes 388
  62.0 27.2 %all-to-all-start = ((bf16[128,32,96]{0,2,1:T(8,128)(2,1)}), bf16[128,32,96]{0,2,1:T(8,128)(2,1)S(1)}, u32[]{:S(2)}, u32[]{:S(2)}) async-start(bf16[128,32,96]{0,2,1:T(8,128)(2,1)} %bitcast.3), calls=%async_computation | async-start | bytes 1572864 | tf_op jit(solution)/shard_map/all_to_all | solution.py:86
  75.8 52.4 %collective-permute-start = (bf16[2,4096,96]{1,2,0:T(8,128)(2,1)}, bf16[2,4096,96]{1,2,0:T(8,128)(2,1)}, u32[]{:S(2)}, u32[]{:S(2)}) collective-permute-start(bf16[2,4096,96]{1,2,0:T(8,128)(2,1)} %pad_maximum_fusion), channel_id=1, source_target_pairs={{0,32},{32,64},{64,96},{96,128},{128,160},{160,192},{192,224},{1,3... | collective-permute-start | bytes 4718600 | tf_op jit(solution)/shard_map/ppermute | solution.py:15
  89.2 38.0 %all-to-all-start.3 = ((bf16[128,32,96]{0,2,1:T(8,128)(2,1)}), bf16[128,32,96]{0,2,1:T(8,128)(2,1)S(1)}, u32[]{:S(2)}, u32[]{:S(2)}) async-start(bf16[128,32,96]{0,2,1:T(8,128)(2,1)} %bitcast.11), calls=%async_computation.3 | async-start | bytes 1572864 | tf_op jit(solution)/shard_map/all_to_all | solution.py:89
  281.4 5.3 %copy-start.4 = (bf16[8,512,96]{1,2,0:T(8,128)(2,1)S(1)}, bf16[8,512,96]{1,2,0:T(8,128)(2,1)}, u32[]{:S(2)}) copy-start(bf16[8,512,96]{1,2,0:T(8,128)(2,1)} %get-tuple-element.181) | copy-start | bytes 2359300
  282.7 46.5 %collective-permute-start.1 = (f32[2,1,2048,96]{2,3,1,0:T(8,128)}, f32[2,1,2048,96]{2,3,1,0:T(8,128)}, u32[]{:S(2)}, u32[]{:S(2)}) collective-permute-start(f32[2,1,2048,96]{2,3,1,0:T(8,128)} %pad_maximum_fusion.1), channel_id=1, source_target_pairs={{32,0},{64,32},{96,64},{128,96},{160,128},{192,160},{224,192},{33,... | collective-permute-start | bytes 4718600 | tf_op jit(solution)/shard_map/ppermute | solution.py:15
  290.8 42.3 %all-to-all-start.4 = ((bf16[32,128,96]{1,2,0:T(8,128)(2,1)}), bf16[32,128,96]{1,2,0:T(8,128)(2,1)S(1)}, u32[]{:S(2)}, u32[]{:S(2)}) async-start(bf16[32,128,96]{1,2,0:T(8,128)(2,1)} %copy.82), calls=%async_computation.4 | async-start | bytes 1572864 | tf_op jit(solution)/shard_map/all_to_all | solution.py:128
  331.0 0.9 copy-start
  333.0 29.5 %all-to-all-start.5 = ((bf16[32,128,96]{1,2,0:T(8,128)(2,1)}), bf16[32,128,96]{1,2,0:T(8,128)(2,1)S(1)}, u32[]{:S(2)}, u32[]{:S(2)}) async-start(bf16[32,128,96]{1,2,0:T(8,128)(2,1)} %copy.83), calls=%async_computation.5 | async-start | bytes 1572864 | tf_op jit(solution)/shard_map/all_to_all | solution.py:129
  362.5 27.3 %all-to-all-start.6 = ((bf16[32,128,96]{1,2,0:T(8,128)(2,1)}), bf16[32,128,96]{1,2,0:T(8,128)(2,1)S(1)}, u32[]{:S(2)}, u32[]{:S(2)}) async-start(bf16[32,128,96]{1,2,0:T(8,128)(2,1)} %copy.84), calls=%async_computation.6 | async-start | bytes 1572864 | tf_op jit(solution)/shard_map/all_to_all | solution.py:130
where the time goes:
time: 396 us; the launch traced here: 391 us
  waiting for transfers between devices  147 us (37%)
  matrix products  100 us (25%)
  starting transfers between devices  57.8 us (15%)
  local copies, waits for them, and re-layouts  46.4 us (12%)
  other arithmetic  32.5 us (8%)
  loops' own time  5.56 us (1%)
    all_to_all x1, waiting for transfers between devices, shards(): lax.all_to_all(out_grad, 'head', split_axis=1, concat_axis=0, tiled=True)  30.7 us
    ppermute x2, waiting for transfers between devices, from_behind(): return lax.ppermute(block, axis, route)  29.4 us
    dot_general x8, matrix products, block_grads(): jnp.dot(weights.T, grad_blk, preferred_element_type=jnp.float32)  23.2 us
    dot_general x8, matrix products, block_grads(): jnp.dot(query_blk, key_win.T, preferred_element_type=jnp.float32) * factor  21.9 us
    dot_general x8, matrix products, block_grads(): jnp.dot(grad_score, key_win, preferred_element_type=jnp.float32) * factor  20.8 us
    all_to_all x1, waiting for transfers between devices, shards(): lax.all_to_all(values, 'head', split_axis=1, concat_axis=0, tiled=True)  20.2 us
    all_to_all x1, waiting for transfers between devices, shards(): lax.all_to_all(keys_in, 'head', split_axis=1, concat_axis=0, tiled=True)  20.1 us
    all_to_all x1, waiting for transfers between devices, shards(): lax.all_to_all(value_out, 'head', split_axis=0, concat_axis=1, tiled=True)  19.1 us
  transfers between devices with their start and end apart: 9, of which 7 were waited for; matrix products, arithmetic and copies ran while one was open for 6% of the time, Pallas kernels for 0%

commit v1 on v0

v1 whole, which is shorter than its diff:
```python
import functools, math
import jax
import jax.numpy as jnp
from jax import lax
from jax.experimental import pallas as pl
from jax.experimental.pallas import tpu as pltpu
from jax.sharding import PartitionSpec as P

HD = 96
CH = 128
CQ = 4
CK = 4
FACTOR = 1.0 / math.sqrt(HD)
LOG2 = FACTOR * math.log2(math.e)


def attend_kernel(spec, lens, base, halo, own, qd, dq, back, mine, kvt, kn, vn, score, acc, oacc, qacc):
    nc, docs, cq, ck, q_row, native = spec
    tq, tk = cq * CH, ck * CH
    span = nc * CH
    first = base[0]
    origin = first - span

    def doc_start(position):
        begin, found = jnp.int32(0), jnp.int32(0)
        for d in range(docs):
            found = jnp.where(begin <= position, begin, found)
            begin = begin + lens[d]
        return found - origin

    low_chunk = doc_start(first) // CH
    low_chunk = (low_chunk // ck) * ck

    def stage_halo(c, _):
        block = halo[c]
        kvt[c] = block
        rows = pl.ds(pl.multiple_of(c * CH, CH), CH)
        kn[rows, :] = block[:HD].T
        vn[rows, :] = block[HD:].T
        acc[c] = jnp.zeros((2 * HD, CH), jnp.float32)
        return 0

    def stage_own(c, _):
        block = own[c, : 2 * HD, :]
        kvt[nc + c] = block
        rows = pl.ds(pl.multiple_of((nc + c) * CH, CH), CH)
        kn[rows, :] = block[:HD].T
        vn[rows, :] = block[HD:].T
        acc[nc + c] = jnp.zeros((2 * HD, CH), jnp.float32)
        return 0

    def clear(c, _):
        acc[c] = jnp.zeros((2 * HD, CH), jnp.float32)
        return 0

    lax.fori_loop(0, jnp.minimum(low_chunk, nc), clear, 0)
    lax.fori_loop(low_chunk, nc, stage_halo, 0)
    lax.fori_loop(0, nc, stage_own, 0)

    def wide(ref, chunk, rows, count):
        return jnp.concatenate([ref[chunk + n, rows, :] for n in range(count)], axis=1)

    def q_step(i, _):
        q_chunk = i * cq
        q_begin = span + i * tq
        begin, lo, hi = jnp.int32(0), jnp.int32(0), jnp.int32(0)
        q_pos = q_begin + lax.broadcasted_iota(jnp.int32, (1, tq), 1)
        start_row = jnp.zeros((1, tq), jnp.int32)
        for d in range(docs):
            here = begin - origin
            lo = jnp.where(here <= q_begin, here, lo)
            hi = jnp.where(here <= q_begin + (tq - 1), here, hi)
            start_row = jnp.where(q_pos >= here, here, start_row)
            begin = begin + lens[d]
        k_first = lo // tk
        k_last = (q_begin + tq - 1) // tk + 1
        qt = wide(qd, q_chunk, pl.ds(q_row, HD), cq)
        gt = wide(qd, q_chunk, pl.ds(q_row + HD, HD), cq)

        def score_step(j, top):
            slot = pl.ds(pl.multiple_of((j - k_first) * tk, tk), tk)
            rows = pl.ds(pl.multiple_of(j * tk, tk), tk)
            k_begin = j * tk
            s = jnp.dot(kn[rows, :], qt, preferred_element_type=jnp.float32)
            plain = (k_begin >= hi) & (k_begin + tk <= q_begin)

            def masked(s):
                k_pos = k_begin + lax.broadcasted_iota(jnp.int32, (tk, tq), 0)
                keep = (k_pos >= start_row) & (k_pos <= q_pos)
                return jnp.where(keep, s, -1e30)

            s = lax.cond(plain, lambda s: s, masked, s) if native else masked(s)
            score[slot, :] = s
            return jnp.maximum(top, jnp.max(s.reshape(tk // 8, 8, tq), axis=0))

        top = lax.fori_loop(k_first, k_last, score_step, jnp.full((8, tq), -1e30, jnp.float32))
        top = jnp.max(top, axis=0, keepdims=True)
        oacc[...] = jnp.zeros_like(oacc)

        def power_step(j, total):
            slot = pl.ds(pl.multiple_of((j - k_first) * tk, tk), tk)
            p = jnp.exp2((score[slot, :] - top) * LOG2)
            score[slot, :] = p
            vt = wide(kvt, j * ck, pl.ds(HD, HD), ck)
            oacc[...] += jnp.dot(vt, p.astype(jnp.bfloat16), preferred_element_type=jnp.float32)
            return total + jnp.sum(p.reshape(tk // 8, 8, tq), axis=0)

        total = lax.fori_loop(k_first, k_last, power_step, jnp.zeros((8, tq), jnp.float32))
        inverse = 1.0 / jnp.sum(total, axis=0, keepdims=True)
        attended = (oacc[...] * inverse).astype(jnp.bfloat16).astype(jnp.float32)
        delta = jnp.sum(gt.astype(jnp.float32) * attended, axis=0, keepdims=True)
        qacc[...] = jnp.zeros_like(qacc)

        def grad_step(j, _):
            slot = pl.ds(pl.multiple_of((j - k_first) * tk, tk), tk)
            rows = pl.ds(pl.multiple_of(j * tk, tk), tk)
            shares = score[slot, :] * inverse
            weights = shares.astype(jnp.bfloat16)
            prob = jnp.dot(vn[rows, :], gt, preferred_element_type=jnp.float32)
            grad = (shares * (prob - delta)).astype(jnp.bfloat16)
            kt = wide(kvt, j * ck, pl.ds(0, HD), ck)
            qacc[...] += jnp.dot(kt, grad, preferred_element_type=jnp.float32)
            last = (((1,), (1,)), ((), ()))
            dk = lax.dot_general(qt, grad, last, preferred_element_type=jnp.float32)
            dv = lax.dot_general(gt, weights, last, preferred_element_type=jnp.float32)
            for n in range(ck):
                cols = slice(n * CH, (n + 1) * CH)
                acc[j * ck + n, :HD, :] += dk[:, cols]
                acc[j * ck + n, HD:, :] += dv[:, cols]
            return 0

        lax.fori_loop(k_first, k_last, grad_step, 0)
        out = (qacc[...] * FACTOR).astype(jnp.bfloat16)
        for n in range(cq):
            dq[q_chunk + n] = out[:, n * CH : (n + 1) * CH]
        return 0

    lax.fori_loop(0, nc // cq, q_step, 0)

    def finish(c, _):
        back[c, :HD, :] = (acc[c, :HD, :] * FACTOR).astype(jnp.bfloat16)
        back[c, HD:, :] = acc[c, HD:, :].astype(jnp.bfloat16)
        mine[c, :HD, :] = acc[nc + c, :HD, :] * FACTOR
        mine[c, HD:, :] = acc[nc + c, HD:, :]
        return 0

    lax.fori_loop(0, nc, finish, 0)


def attend(lens, base, halo, own, qd, q_row, cq=2, ck=2, native=True):
    nc = halo.shape[0]
    tq, tk = cq * CH, ck * CH
    window = nc * CH + tq + tk
    spec = (nc, lens.shape[0], cq, ck, q_row, native)
    smem = pl.BlockSpec(memory_space=pltpu.SMEM)
    vmem = pl.BlockSpec(memory_space=pltpu.VMEM)
    return pl.pallas_call(
        functools.partial(attend_kernel, spec),
        out_shape=(
            jax.ShapeDtypeStruct((nc, HD, CH), jnp.bfloat16),
            jax.ShapeDtypeStruct((nc, 2 * HD, CH), jnp.bfloat16),
            jax.ShapeDtypeStruct((nc, 2 * HD, CH), jnp.float32),
        ),
        in_specs=[smem, smem, vmem, vmem, vmem],
        out_specs=(vmem, vmem, vmem),
        scratch_shapes=[
            pltpu.VMEM((2 * nc, 2 * HD, CH), jnp.bfloat16),
            pltpu.VMEM((2 * nc * CH, HD), jnp.bfloat16),
            pltpu.VMEM((2 * nc * CH, HD), jnp.bfloat16),
            pltpu.VMEM((window, tq), jnp.float32),
            pltpu.VMEM((2 * nc, 2 * HD, CH), jnp.float32),
            pltpu.VMEM((HD, tq), jnp.float32),
            pltpu.VMEM((HD, tq), jnp.float32),
        ],
        compiler_params=pltpu.CompilerParams(vmem_limit_bytes=40 * 1024 * 1024),
        name="attend",
    )(lens, base, halo, own, qd)


def pack_kernel(plan, *refs):
    ins, outs = refs[:4], refs[4:]
    for source, (which, row) in zip(ins, plan):
        for m in range(source.shape[1] // (4 * HD)):
            block = source[:, m * 4 * HD : (m + 1) * 4 * HD].T
            for n in range(4):
                outs[which][4 * m + n, row : row + HD, :] = block[n * HD : (n + 1) * HD]


def pack(arrays, half, plan, rows):
    tokens, columns = arrays[0].shape
    half_columns = columns // 2
    peers = half_columns // HD
    return pl.pallas_call(
        functools.partial(pack_kernel, plan),
        grid=(1,),
        out_shape=tuple(jax.ShapeDtypeStruct((peers, r, tokens), jnp.bfloat16) for r in rows),
        in_specs=[pl.BlockSpec((tokens, half_columns), lambda i: (0, half))] * 4,
        out_specs=tuple(pl.BlockSpec((peers, r, tokens), lambda i: (0, 0, 0)) for r in rows),
        compiler_params=pltpu.CompilerParams(vmem_limit_bytes=32 * 1024 * 1024),
        name="pack",
    )(*arrays)


def unpack_kernel(plan, n_in, n_pass, *refs):
    ins, outs = refs[:n_in], refs[n_in + n_pass :]
    for target, (which, row) in zip(outs, plan):
        for m in range(target.shape[1] // (4 * HD)):
            parts = [ins[which][4 * m + n, row : row + HD, :] for n in range(4)]
            target[:, m * 4 * HD : (m + 1) * 4 * HD] = jnp.concatenate(parts, axis=0).T


def unpack(received, half, plan, earlier=()):
    peers, _, tokens = received[0].shape
    columns = 2 * peers * HD
    shape = jax.ShapeDtypeStruct((tokens, columns), jnp.bfloat16)
    n_in, n_pass = len(received), len(earlier)
    return pl.pallas_call(
        functools.partial(unpack_kernel, plan, n_in, n_pass),
        grid=(1,),
        out_shape=(shape,) * len(plan),
        in_specs=[pl.BlockSpec(r.shape, lambda i: (0, 0, 0)) for r in received]
        + [pl.BlockSpec(memory_space=pl.ANY)] * n_pass,
        out_specs=(pl.BlockSpec((tokens, columns // 2), lambda i: (0, half)),) * len(plan),
        input_output_aliases={n_in + n: n for n in range(n_pass)},
        compiler_params=pltpu.CompilerParams(vmem_limit_bytes=32 * 1024 * 1024),
        name="unpack",
    )(*received, *earlier)


def total_kernel(extra, *refs):
    mine, got, out = refs[extra], refs[extra + 1], refs[-1]
    if extra:
        out[:, :HD, :] = refs[0][...]
    base = HD if extra else 0
    out[:, base:, :] = (mine[...] + got[...].astype(jnp.float32)).astype(jnp.bfloat16)


def total(first, mine, got):
    peers, rows, tokens = mine.shape
    extra = len(first)
    return pl.pallas_call(
        functools.partial(total_kernel, extra),
        out_shape=jax.ShapeDtypeStruct((peers, rows + HD * extra, tokens), jnp.bfloat16),
        in_specs=[pl.BlockSpec(memory_space=pltpu.VMEM)] * (2 + extra),
        out_specs=pl.BlockSpec(memory_space=pltpu.VMEM),
        compiler_params=pltpu.CompilerParams(vmem_limit_bytes=32 * 1024 * 1024),
        name="total",
    )(*first, mine, got)


def shards(queries, keys_in, values, out_grad, doc_lengths):
    blocks, group = lax.axis_size("blk"), lax.axis_size("head") // 2
    tokens = queries.shape[0]
    devices = 2 * blocks * group
    halves = [list(range(group)), list(range(group, 2 * group))]
    up = [(i, i + group) for i in range(devices - group)]
    down = [(i + group, i) for i in range(devices - group)]

    def exchange(x):
        return lax.all_to_all(
            x, "head", split_axis=0, concat_axis=0, tiled=True, axis_index_groups=halves
        )

    def shift(x, route):
        return lax.ppermute(x, ("blk", "head"), route)

    def after(x, *earlier):
        return lax.optimization_barrier((x, *earlier))[0]

    half_index = lax.axis_index("blk") * 2 + lax.axis_index("head") // group
    base = (half_index * (group * tokens)).astype(jnp.int32).reshape(1)
    arrays = (keys_in, values, queries, out_grad)
    (send_a,) = pack(arrays, 0, ((0, 0), (0, HD), (0, 2 * HD), (0, 3 * HD)), (4 * HD,))
    send_kv, send_qd = pack(arrays, 1, ((0, 0), (0, HD), (1, 0), (1, HD)), (2 * HD, 2 * HD))

    own_a = exchange(send_a)
    halo_a = shift(own_a[:, : 2 * HD, :], up)
    own_b = exchange(after(send_kv, own_a))
    halo_b = shift(own_b, up)
    rows_b = exchange(after(send_qd, own_b, halo_a))

    dq_a, back_a, mine_a = attend(doc_lengths, base, after(halo_a, own_b), own_a, own_a, 2 * HD, CQ, CK, False)
    got_a = shift(back_a, down)
    out_qa = exchange(after(dq_a, rows_b, halo_b))
    dq_b, back_b, mine_b = attend(doc_lengths, base, halo_b, own_b, rows_b, 0, CQ, CK, False)
    got_b = shift(back_b, down)
    out_ab = exchange(after(total((dq_b,), mine_a, got_a), out_qa))
    out_b = exchange(after(total((), mine_b, got_b), out_ab))
    early = unpack((out_qa, out_ab), 0, ((0, 0), (1, HD), (1, 2 * HD)))
    return unpack((out_ab, out_b), 1, ((0, 0), (1, 0), (1, HD)), early)


def solution(mesh):
    rows = P(("blk", "head"), None)
    return jax.shard_map(
        shards,
        mesh=mesh,
        in_specs=(rows, rows, rows, rows, P()),
        out_specs=(rows, rows, rows),
        check_vma=False,
    )
```

time: 396 us -> 224 us (0.57)
  the two profiles are of different devices: /device:TPU:17 before, /device:TPU:5 now
where the time goes in v1:
time: 224 us; the launch traced here: 220 us
  waiting for transfers between devices  102 us (46%)
  Pallas kernels  54.9 us (25%)
  starting transfers between devices  48.7 us (22%)
  local copies, waits for them, and re-layouts  13.8 us (6%)
    all_to_all x6, waiting for transfers between devices, exchange(): lax.all_to_all(x, 'head', split_axis=0, concat_axis=0, tiled=True, axis_i...  64.5 us
    pallas_call x2, Pallas kernels, attend(): pl.pallas_call(functools.partial(attend_kernel, spec), out_shape=(jax.Sha...  47.1 us
    all_to_all x6, starting transfers between devices, exchange(): lax.all_to_all(x, 'head', split_axis=0, concat_axis=0, tiled=True, axis_i...  39.2 us
    ppermute x4, waiting for transfers between devices, shift(): return lax.ppermute(x, ('blk', 'head'), route)  37.4 us
    unnamed x38, local copies, waits for them, and re-layouts  13.8 us
    ppermute x4, starting transfers between devices, shift(): return lax.ppermute(x, ('blk', 'head'), route)  9.51 us
  transfers between devices with their start and end apart: 10, of which 6 were waited for; matrix products, arithmetic and copies ran while one was open for 0% of the time, Pallas kernels for 24%

profile of v1, /device:TPU:5, one launch (start us, length us, event | category | flops | bytes accessed | tf_op | source)
XLA Modules:
  0.0 220.2 jit_solution(17101048338516493568)
XLA Ops:
  0.6 1.1 copy-done
  1.8 1.1 copy-done.2
  2.9 1.1 copy-done.4
  4.0 1.1 copy-done.6
  5.2 1.7 pack.3
  6.8 9.3 %all-to-all-start = ((bf16[16,384,128]{2,1,0:T(8,128)(2,1)}), bf16[16,384,128]{2,1,0:T(8,128)(2,1)S(1)}, u32[]{:S(2)}, u32[]{:S(2)}) async-start(bf16[16,384,128]{2,1,0:T(8,128)(2,1)} %pack.3), calls=%async_computation | async-start | bytes 3145728 | tf_op jit(solution)/shard_map/all_to_all | solution.py:260
  16.1 1.1 copy-done.5
  17.3 1.1 copy-done.7
  20.6 33.9 %all-to-all-done.own.qd = bf16[16,384,128]{2,1,0:T(8,128)(2,1)S(1)} async-done(((bf16[16,384,128]{2,1,0:T(8,128)(2,1)}), bf16[16,384,128]{2,1,0:T(8,128)(2,1)S(1)}, u32[]{:S(2)}, u32[]{:S(2)}) %all-to-all-start) | async-done | bytes 1572896 | tf_op jit(solution)/shard_map/all_to_all | solution.py:260
  54.5 4.3 %all-to-all-start.1 = ((bf16[16,192,128]{2,1,0:T(8,128)(2,1)}), bf16[16,192,128]{2,1,0:T(8,128)(2,1)S(1)}, u32[]{:S(2)}, u32[]{:S(2)}) async-start(bf16[16,192,128]{2,1,0:T(8,128)(2,1)} %copy-done.13), calls=%async_computation.1 | async-start | bytes 1572864 | tf_op jit(solution)/shard_map/all_to_all | solution.py:260
  58.9 2.8 %collective-permute-start.1 = (bf16[16,192,128]{2,1,0:T(8,128)(2,1)S(1)}, bf16[16,192,128]{2,1,0:T(8,128)(2,1)S(1)}, u32[]{:S(2)}, u32[]{:S(2)}) collective-permute-start(bf16[16,192,128]{2,1,0:T(8,128)(2,1)S(1)} %slice.4), channel_id=1, source_target_pairs={{0,16},{1,17},{2,18},{3,19},{4,20},{5,21},{6,22},{7,23},{8,24},{9,... | collective-permute-start | bytes 2359304 | tf_op jit(solution)/shard_map/ppermute | solution.py:265
  61.7 18.1 %collective-permute-done.1.halo = bf16[16,192,128]{2,1,0:T(8,128)(2,1)S(1)} collective-permute-done((bf16[16,192,128]{2,1,0:T(8,128)(2,1)S(1)}, bf16[16,192,128]{2,1,0:T(8,128)(2,1)S(1)}, u32[]{:S(2)}, u32[]{:S(2)}) %collective-permute-start.1) | collective-permute-done | bytes 786464 | tf_op jit(solution)/shard_map/ppermute | solution.py:265
  79.9 0.9 copy-done.14
  81.5 7.0 %all-to-all-start.2 = ((bf16[16,192,128]{2,1,0:T(8,128)(2,1)}), bf16[16,192,128]{2,1,0:T(8,128)(2,1)S(1)}, u32[]{:S(2)}, u32[]{:S(2)}) async-start(bf16[16,192,128]{2,1,0:T(8,128)(2,1)} %copy-done.12), calls=%async_computation.2 | async-start | bytes 1572864 | tf_op jit(solution)/shard_map/all_to_all | solution.py:260
  88.5 2.8 %collective-permute-start = (bf16[16,192,128]{2,1,0:T(8,128)(2,1)S(1)}, bf16[16,192,128]{2,1,0:T(8,128)(2,1)}, u32[]{:S(2)}, u32[]{:S(2)}) collective-permute-start(bf16[16,192,128]{2,1,0:T(8,128)(2,1)S(1)} %all-to-all-done.1.own), channel_id=1, source_target_pairs={{0,16},{1,17},{2,18},{3,19},{4,20},{5,21},{6,22},{7,23},{8,24},{9,... | collective-permute-start | bytes 2359304 | tf_op jit(solution)/shard_map/ppermute | solution.py:265
  91.4 1.1 copy-done.15
  92.5 23.7 %attend.3 = (bf16[16,96,128]{2,1,0:T(8,128)(2,1)S(1)}, bf16[16,192,128]{2,1,0:T(8,128)(2,1)}, f32[16,192,128]{2,1,0:T(8,128)S(1)}) custom-call(s32[32]{0:T(128)S(1)} %copy-done.17, s32[1]{0:T(128)} %bitcast.base, bf16[16,192,128]{2,1,0:T(8,128)(2,1)S(1)} %copy-done.15, bf16[16,384,128]{2,1,0:T(8,128)(2,1)S(1)} %all-to-all-done.own.qd, ...), custom_call_target="tpu_custom_call" | custom-call | tf_op jit(solution)/shard_map/attend/pallas_call | solution.py:157
  116.2 1.2 copy-done.10
  117.4 1.9 collective-permute-start.2
  119.4 7.6 %all-to-all-start.3 = ((bf16[16,96,128]{2,1,0:T(8,128)(2,1)}), bf16[16,96,128]{2,1,0:T(8,128)(2,1)S(1)}, u32[]{:S(2)}, u32[]{:S(2)}) async-start(bf16[16,96,128]{2,1,0:T(8,128)(2,1)} %copy-done.16), calls=%async_computation.3 | async-start | bytes 786432 | tf_op jit(solution)/shard_map/all_to_all | solution.py:260
  127.0 23.4 %attend.2 = (bf16[16,96,128]{2,1,0:T(8,128)(2,1)S(1)}, bf16[16,192,128]{2,1,0:T(8,128)(2,1)S(1)}, f32[16,192,128]{2,1,0:T(8,128)S(1)}) custom-call(s32[32]{0:T(128)S(1)} %copy-done.17, s32[1]{0:T(128)} %bitcast.base, bf16[16,192,128]{2,1,0:T(8,128)(2,1)} %collective-permute-done.halo, bf16[16,192,128]{2,1,0:T(8,128)(2,1)S(1)} %all-to-all-done.1.own, ...), custom_call_target="tpu_custom_call" | custom-call | tf_op jit(solution)/shard_map/attend/pallas_call | solution.py:157
  150.4 1.1 copy-done.8
  152.4 2.3 %total.2 = bf16[16,288,128]{2,1,0:T(8,128)(2,1)} custom-call(bf16[16,96,128]{2,1,0:T(8,128)(2,1)S(1)} %get-tuple-element.24.refs_0_, f32[16,192,128]{2,1,0:T(8,128)S(1)} %copy-done.11, bf16[16,192,128]{2,1,0:T(8,128)(2,1)} %collective-permute-done.2.refs_2_), custom_call_target="tpu_custom_call" | custom-call | tf_op jit(solution)/shard_map/total/pallas_call | solution.py:241
  154.8 7.4 %all-to-all-start.4 = ((bf16[16,288,128]{2,1,0:T(8,128)(2,1)}), bf16[16,288,128]{2,1,0:T(8,128)(2,1)S(1)}, u32[]{:S(2)}, u32[]{:S(2)}) async-start(bf16[16,288,128]{2,1,0:T(8,128)(2,1)} %total.2), calls=%async_computation.4 | async-start | bytes 2359296 | tf_op jit(solution)/shard_map/all_to_all | solution.py:260
  162.1 1.9 collective-permute-start.3
  164.0 19.3 %collective-permute-done.3.refs_1_ = bf16[16,192,128]{2,1,0:T(8,128)(2,1)S(1)} collective-permute-done((bf16[16,192,128]{2,1,0:T(8,128)(2,1)}, bf16[16,192,128]{2,1,0:T(8,128)(2,1)S(1)}, u32[]{:S(2)}, u32[]{:S(2)}) %collective-permute-start.3) | collective-permute-done | bytes 786464 | tf_op jit(solution)/shard_map/ppermute | solution.py:265
  183.3 1.0 total.3
  184.3 8.3 %all-to-all-done.4.refs_1_.refs_0_ = bf16[16,288,128]{2,1,0:T(8,128)(2,1)S(1)} async-done(((bf16[16,288,128]{2,1,0:T(8,128)(2,1)}), bf16[16,288,128]{2,1,0:T(8,128)(2,1)S(1)}, u32[]{:S(2)}, u32[]{:S(2)}) %all-to-all-start.4) | async-done | bytes 1179680 | tf_op jit(solution)/shard_map/all_to_all | solution.py:260
  192.7 3.7 %all-to-all-start.5 = ((bf16[16,192,128]{2,1,0:T(8,128)(2,1)}), bf16[16,192,128]{2,1,0:T(8,128)(2,1)S(1)}, u32[]{:S(2)}, u32[]{:S(2)}) async-start(bf16[16,192,128]{2,1,0:T(8,128)(2,1)} %total.3), calls=%async_computation.5 | async-start | bytes 1572864 | tf_op jit(solution)/shard_map/all_to_all | solution.py:260
  196.4 1.2 unpack.2
  197.6 21.5 %all-to-all-done.5.refs_1_ = bf16[16,192,128]{2,1,0:T(8,128)(2,1)S(1)} async-done(((bf16[16,192,128]{2,1,0:T(8,128)(2,1)}), bf16[16,192,128]{2,1,0:T(8,128)(2,1)S(1)}, u32[]{:S(2)}, u32[]{:S(2)}) %all-to-all-start.5) | async-done | bytes 786464 | tf_op jit(solution)/shard_map/all_to_all | solution.py:260
  219.1 1.2 unpack.3
  (35 shorter events, 3.9 us)
Async XLA Ops:
  0.6 1.1 copy-start
  1.8 1.1 copy-start.2
  2.9 1.1 copy-start.4
  4.0 1.1 copy-start.6
  6.8 9.3 %copy-start.1 = (bf16[128,3072]{1,0:T(8,128)(2,1)S(1)}, bf16[128,3072]{1,0:T(8,128)(2,1)}, u32[]{:S(2)}) copy-start(bf16[128,3072]{1,0:T(8,128)(2,1)} %refs_0_.3) | copy-start | bytes 2359300
  6.8 9.3 %copy-start.3 = (bf16[128,3072]{1,0:T(8,128)(2,1)S(1)}, bf16[128,3072]{1,0:T(8,128)(2,1)}, u32[]{:S(2)}) copy-start(bf16[128,3072]{1,0:T(8,128)(2,1)} %refs_1_.3) | copy-start | bytes 2359300
  6.8 47.7 %all-to-all-start = ((bf16[16,384,128]{2,1,0:T(8,128)(2,1)}), bf16[16,384,128]{2,1,0:T(8,128)(2,1)S(1)}, u32[]{:S(2)}, u32[]{:S(2)}) async-start(bf16[16,384,128]{2,1,0:T(8,128)(2,1)} %pack.3), calls=%async_computation | async-start | bytes 3145728 | tf_op jit(solution)/shard_map/all_to_all | solution.py:260
  16.1 1.1 copy-start.5
  17.3 1.1 copy-start.7
  18.9 0.9 copy-start.12
  19.7 0.9 copy-start.13
  54.5 26.9 %all-to-all-start.1 = ((bf16[16,192,128]{2,1,0:T(8,128)(2,1)}), bf16[16,192,128]{2,1,0:T(8,128)(2,1)S(1)}, u32[]{:S(2)}, u32[]{:S(2)}) async-start(bf16[16,192,128]{2,1,0:T(8,128)(2,1)} %copy-done.13), calls=%async_computation.1 | async-start | bytes 1572864 | tf_op jit(solution)/shard_map/all_to_all | solution.py:260
  58.8 32.5 %copy-start.17 = (s32[32]{0:T(128)S(1)}, s32[32]{0:T(128)}, u32[]{:S(2)}) copy-start(s32[32]{0:T(128)} %lens.3) | copy-start | bytes 388
  58.9 21.0 %collective-permute-start.1 = (bf16[16,192,128]{2,1,0:T(8,128)(2,1)S(1)}, bf16[16,192,128]{2,1,0:T(8,128)(2,1)S(1)}, u32[]{:S(2)}, u32[]{:S(2)}) collective-permute-start(bf16[16,192,128]{2,1,0:T(8,128)(2,1)S(1)} %slice.4), channel_id=1, source_target_pairs={{0,16},{1,17},{2,18},{3,19},{4,20},{5,21},{6,22},{7,23},{8,24},{9,... | collective-permute-start | bytes 2359304 | tf_op jit(solution)/shard_map/ppermute | solution.py:265
  79.9 0.9 copy-start.14
  81.5 37.9 %all-to-all-start.2 = ((bf16[16,192,128]{2,1,0:T(8,128)(2,1)}), bf16[16,192,128]{2,1,0:T(8,128)(2,1)S(1)}, u32[]{:S(2)}, u32[]{:S(2)}) async-start(bf16[16,192,128]{2,1,0:T(8,128)(2,1)} %copy-done.12), calls=%async_computation.2 | async-start | bytes 1572864 | tf_op jit(solution)/shard_map/all_to_all | solution.py:260
  88.5 30.8 %collective-permute-start = (bf16[16,192,128]{2,1,0:T(8,128)(2,1)S(1)}, bf16[16,192,128]{2,1,0:T(8,128)(2,1)}, u32[]{:S(2)}, u32[]{:S(2)}) collective-permute-start(bf16[16,192,128]{2,1,0:T(8,128)(2,1)S(1)} %all-to-all-done.1.own), channel_id=1, source_target_pairs={{0,16},{1,17},{2,18},{3,19},{4,20},{5,21},{6,22},{7,23},{8,24},{9,... | collective-permute-start | bytes 2359304 | tf_op jit(solution)/shard_map/ppermute | solution.py:265
  91.4 1.1 copy-start.15
  116.2 1.2 copy-start.10
  117.4 1.9 copy-start.16
  117.4 34.2 %collective-permute-start.2 = (bf16[16,192,128]{2,1,0:T(8,128)(2,1)}, bf16[16,192,128]{2,1,0:T(8,128)(2,1)}, u32[]{:S(2)}, u32[]{:S(2)}) collective-permute-start(bf16[16,192,128]{2,1,0:T(8,128)(2,1)} %get-tuple-element.27), channel_id=1, source_target_pairs={{16,0},{17,1},{18,2},{19,3},{20,4},{21,5},{22,6},{23,7},{24,8},{25... | collective-permute-start | bytes 2359304 | tf_op jit(solution)/shard_map/ppermute | solution.py:265
  119.3 33.1 %copy-start.11 = (f32[16,192,128]{2,1,0:T(8,128)S(1)}, f32[16,192,128]{2,1,0:T(8,128)}, u32[]{:S(2)}) copy-start(f32[16,192,128]{2,1,0:T(8,128)} %copy-done.10) | copy-start | bytes 4718596
  119.4 35.4 %all-to-all-start.3 = ((bf16[16,96,128]{2,1,0:T(8,128)(2,1)}), bf16[16,96,128]{2,1,0:T(8,128)(2,1)S(1)}, u32[]{:S(2)}, u32[]{:S(2)}) async-start(bf16[16,96,128]{2,1,0:T(8,128)(2,1)} %copy-done.16), calls=%async_computation.3 | async-start | bytes 786432 | tf_op jit(solution)/shard_map/all_to_all | solution.py:260
  150.4 1.2 copy-start.8
  151.5 0.9 copy-start.18
  154.8 28.6 %copy-start.9 = (f32[16,192,128]{2,1,0:T(8,128)S(1)}, f32[16,192,128]{2,1,0:T(8,128)}, u32[]{:S(2)}) copy-start(f32[16,192,128]{2,1,0:T(8,128)} %copy-done.8) | copy-start | bytes 4718596
  154.8 37.9 %all-to-all-start.4 = ((bf16[16,288,128]{2,1,0:T(8,128)(2,1)}), bf16[16,288,128]{2,1,0:T(8,128)(2,1)S(1)}, u32[]{:S(2)}, u32[]{:S(2)}) async-start(bf16[16,288,128]{2,1,0:T(8,128)(2,1)} %total.2), calls=%async_computation.4 | async-start | bytes 2359296 | tf_op jit(solution)/shard_map/all_to_all | solution.py:260
  162.1 21.2 %collective-permute-start.3 = (bf16[16,192,128]{2,1,0:T(8,128)(2,1)}, bf16[16,192,128]{2,1,0:T(8,128)(2,1)S(1)}, u32[]{:S(2)}, u32[]{:S(2)}) collective-permute-start(bf16[16,192,128]{2,1,0:T(8,128)(2,1)} %copy-done.18), channel_id=1, source_target_pairs={{16,0},{17,1},{18,2},{19,3},{20,4},{21,5},{22,6},{23,7},{24,8},{25... | collective-permute-start | bytes 2359304 | tf_op jit(solution)/shard_map/ppermute | solution.py:265
  192.7 26.4 %all-to-all-start.5 = ((bf16[16,192,128]{2,1,0:T(8,128)(2,1)}), bf16[16,192,128]{2,1,0:T(8,128)(2,1)S(1)}, u32[]{:S(2)}, u32[]{:S(2)}) async-start(bf16[16,192,128]{2,1,0:T(8,128)(2,1)} %total.3), calls=%async_computation.5 | async-start | bytes 1572864 | tf_op jit(solution)/shard_map/all_to_all | solution.py:260

commit v2 on v1

v2 whole, which is shorter than its diff:
```python
import functools, math
import jax
import jax.numpy as jnp
from jax import lax
from jax.experimental import pallas as pl
from jax.experimental.pallas import tpu as pltpu
from jax.sharding import PartitionSpec as P

HD = 96
CH = 128
CQ = 4
CK = 2
PACK_VMEM = 56 * 1024 * 1024
TOTAL_VMEM = 16 * 1024 * 1024
SUB = 2
RUNS = (4, 2, 1)
ATTEND_VMEM = 40 * 1024 * 1024
FACTOR = 1.0 / math.sqrt(HD)
LOG2 = FACTOR * math.log2(math.e)


def attend_kernel(spec, lens, base, halo, own, qd, *refs):
    dq, back, mine = refs[-10:-7]
    (kvt, kn, vn, score, acc, oacc, qacc) = refs[-7:]
    nc, docs, cq, ck, q_row, native = spec
    tq, tk = cq * CH, ck * CH
    span = nc * CH
    first = base[0]
    origin = first - span

    def doc_start(position):
        begin, found = jnp.int32(0), jnp.int32(0)
        for d in range(docs):
            found = jnp.where(begin <= position, begin, found)
            begin = begin + lens[d]
        return found - origin

    low_chunk = doc_start(first) // CH
    low_chunk = (low_chunk // ck) * ck

    def stage_halo(c, _):
        block = halo[c]
        kvt[c] = block
        rows = pl.ds(pl.multiple_of(c * CH, CH), CH)
        kn[rows, :] = block[:HD].T
        vn[rows, :] = block[HD:].T
        acc[c] = jnp.zeros((2 * HD, CH), jnp.float32)
        return 0

    def stage_own(c, _):
        block = own[c, : 2 * HD, :]
        kvt[nc + c] = block
        rows = pl.ds(pl.multiple_of((nc + c) * CH, CH), CH)
        kn[rows, :] = block[:HD].T
        vn[rows, :] = block[HD:].T
        acc[nc + c] = jnp.zeros((2 * HD, CH), jnp.float32)
        return 0

    def clear(c, _):
        acc[c] = jnp.zeros((2 * HD, CH), jnp.float32)
        return 0

    step = pl.program_id(0)

    @pl.when(step == 0)
    def _():
        lax.fori_loop(0, jnp.minimum(low_chunk, nc), clear, 0)
        lax.fori_loop(low_chunk, nc, stage_halo, 0)
        lax.fori_loop(0, nc, stage_own, 0, unroll=2)


    def wide(ref, chunk, rows, count):
        return jnp.concatenate([ref[chunk + n, rows, :] for n in range(count)], axis=1)

    def q_step(i):
        q_chunk = i * cq
        q_begin = span + i * tq
        begin, lo, hi = jnp.int32(0), jnp.int32(0), jnp.int32(0)
        q_pos = q_begin + lax.broadcasted_iota(jnp.int32, (1, tq), 1)
        start_row = jnp.zeros((1, tq), jnp.int32)
        for d in range(docs):
            here = begin - origin
            lo = jnp.where(here <= q_begin, here, lo)
            hi = jnp.where(here <= q_begin + (tq - 1), here, hi)
            start_row = jnp.where(q_pos >= here, here, start_row)
            begin = begin + lens[d]
        k_first = lo // tk
        k_last = (q_begin + tq - 1) // tk + 1
        qt = wide(qd, q_chunk, pl.ds(q_row, HD), cq)
        gt = wide(qd, q_chunk, pl.ds(q_row + HD, HD), cq)

        def rows_of(j, n):
            return pl.ds(pl.multiple_of(j * tk + n * CH * SUB, CH * SUB), CH * SUB)

        def slot_of(j, n):
            return pl.ds(pl.multiple_of((j - k_first) * tk + n * CH * SUB, CH * SUB), CH * SUB)

        size = CH * SUB

        def sweep(step, carry):
            j = k_first
            for run in RUNS:
                count = (k_last - j) // run
                parts = run * ck // SUB
                carry = lax.fori_loop(0, count, lambda t, c: step(j + t * run, parts, c), carry)
                j = j + count * run
            return carry

        def score_step(j, parts, top):
            def product(n):
                return jnp.dot(kn[rows_of(j, n), :], qt, preferred_element_type=jnp.float32)

            s = product(0)
            for n in range(parts):
                later = product(n + 1) if n + 1 < parts else None
                k_pos = j * tk + n * size + lax.broadcasted_iota(jnp.int32, (size, tq), 0)
                s = jnp.where((k_pos >= start_row) & (k_pos <= q_pos), s, -1e30)
                score[slot_of(j, n), :] = s
                top = jnp.maximum(top, jnp.max(s.reshape(size // 8, 8, tq), axis=0))
                s = later
            return top

        top = sweep(score_step, jnp.full((8, tq), -1e30, jnp.float32))
        top = jnp.max(top, axis=0, keepdims=True)
        oacc[...] = jnp.zeros_like(oacc)

        def power_step(j, parts, total):
            out, held = None, None
            for n in range(parts + 1):
                if n < parts:
                    p = jnp.exp2((score[slot_of(j, n), :] - top) * LOG2)
                    score[slot_of(j, n), :] = p
                    total = total + jnp.sum(p.reshape(size // 8, 8, tq), axis=0)
                    narrow = p.astype(jnp.bfloat16)
                if n:
                    vt = wide(kvt, j * ck + (n - 1) * SUB, pl.ds(HD, HD), SUB)
                    term = jnp.dot(vt, held, preferred_element_type=jnp.float32)
                    out = term if out is None else out + term
                held = narrow
            oacc[...] += out
            return total

        total = sweep(power_step, jnp.zeros((8, tq), jnp.float32))
        inverse = 1.0 / jnp.sum(total, axis=0, keepdims=True)
        attended = (oacc[...] * inverse).astype(jnp.bfloat16).astype(jnp.float32)
        delta = jnp.sum(gt.astype(jnp.float32) * attended, axis=0, keepdims=True)
        qacc[...] = jnp.zeros_like(qacc)

        def grad_step(j, parts, _):
            last = (((1,), (1,)), ((), ()))

            def product(n):
                return jnp.dot(vn[rows_of(j, n), :], gt, preferred_element_type=jnp.float32)

            prob, held, out = product(0), None, None
            for n in range(parts + 1):
                later = product(n + 1) if n + 1 < parts else None
                if n < parts:
                    shares = score[slot_of(j, n), :] * inverse
                    weights = shares.astype(jnp.bfloat16)
                    grad = (shares * (prob - delta)).astype(jnp.bfloat16)
                if n:
                    old_weights, old_grad = held
                    m = j * ck + (n - 1) * SUB
                    kt = wide(kvt, m, pl.ds(0, HD), SUB)
                    term = jnp.dot(kt, old_grad, preferred_element_type=jnp.float32)
                    out = term if out is None else out + term
                    dk = lax.dot_general(qt, old_grad, last, preferred_element_type=jnp.float32)
                    dv = lax.dot_general(gt, old_weights, last, preferred_element_type=jnp.float32)
                    for c in range(SUB):
                        cols = slice(c * CH, (c + 1) * CH)
                        acc[m + c, :HD, :] += dk[:, cols]
                        acc[m + c, HD:, :] += dv[:, cols]
                held = (weights, grad)
                prob = later
            qacc[...] += out
            return 0

        sweep(grad_step, 0)
        out = (qacc[...] * FACTOR).astype(jnp.bfloat16)
        for n in range(cq):
            dq[n] = out[:, n * CH : (n + 1) * CH]
            done = acc[i * cq + n]
            back[n, :HD, :] = (done[:HD] * FACTOR).astype(jnp.bfloat16)
            back[n, HD:, :] = done[HD:].astype(jnp.bfloat16)

    q_step(step)

    @pl.when(step == nc // cq - 1)
    def _():
        def finish(c, _):
            mine[c, :HD, :] = acc[nc + c, :HD, :] * FACTOR
            mine[c, HD:, :] = acc[nc + c, HD:, :]
            return 0

        lax.fori_loop(0, nc, finish, 0, unroll=2)


def attend(lens, base, halo, own, qd, q_row, cq=2, ck=2, native=True, carried=()):
    nc = halo.shape[0]
    tq, tk = cq * CH, ck * CH
    window = nc * CH + tq + tk
    spec = (nc, lens.shape[0], cq, ck, q_row, native)
    smem = pl.BlockSpec(memory_space=pltpu.SMEM)

    def whole(x):
        return pl.BlockSpec(x.shape, lambda i: (0, 0, 0))

    def part(rows):
        return pl.BlockSpec((cq, rows, CH), lambda i: (i, 0, 0))

    through = [pl.BlockSpec(memory_space=pl.ANY)] * len(carried)
    return pl.pallas_call(
        functools.partial(attend_kernel, spec),
        grid=(nc // cq,),
        out_shape=tuple(jax.ShapeDtypeStruct(x.shape, x.dtype) for x in carried)
        + (
            jax.ShapeDtypeStruct((nc, HD, CH), jnp.bfloat16),
            jax.ShapeDtypeStruct((nc, 2 * HD, CH), jnp.bfloat16),
            jax.ShapeDtypeStruct((nc, 2 * HD, CH), jnp.float32),
        ),
        in_specs=[smem, smem, whole(halo), whole(own), whole(qd)] + through,
        input_output_aliases={5 + n: n for n in range(len(carried))},
        out_specs=tuple(through)
        + (
            part(HD),
            part(2 * HD),
            pl.BlockSpec((nc, 2 * HD, CH), lambda i: (0, 0, 0)),
        ),
        scratch_shapes=[
            pltpu.VMEM((2 * nc, 2 * HD, CH), jnp.bfloat16),
            pltpu.VMEM((2 * nc * CH, HD), jnp.bfloat16),
            pltpu.VMEM((2 * nc * CH, HD), jnp.bfloat16),
            pltpu.VMEM((window, tq), jnp.float32),
            pltpu.VMEM((2 * nc, 2 * HD, CH), jnp.float32),
            pltpu.VMEM((HD, tq), jnp.float32),
            pltpu.VMEM((HD, tq), jnp.float32),
        ],
        compiler_params=pltpu.CompilerParams(vmem_limit_bytes=ATTEND_VMEM),
        name="attend",
    )(lens, base, halo, own, qd, *carried)


def pack_kernel(plan, *refs):
    ins, outs = refs[: len(plan)], refs[len(plan) :]
    for source, (which, row) in zip(ins, plan):
        for m in range(source.shape[1] // (4 * HD)):
            block = source[:, m * 4 * HD : (m + 1) * 4 * HD].T
            for n in range(4):
                outs[which][4 * m + n, row : row + HD, :] = block[n * HD : (n + 1) * HD]


def pack(arrays, half, plan, rows):
    tokens, columns = arrays[0].shape
    peers = columns // (2 * HD)
    steps = peers // 4
    return pl.pallas_call(
        functools.partial(pack_kernel, plan),
        grid=(steps,),
        out_shape=tuple(jax.ShapeDtypeStruct((peers, r, tokens), jnp.bfloat16) for r in rows),
        in_specs=[pl.BlockSpec((tokens, 4 * HD), lambda i: (0, half * steps + i))] * len(arrays),
        out_specs=tuple(pl.BlockSpec((4, r, tokens), lambda i: (i, 0, 0)) for r in rows),
        compiler_params=pltpu.CompilerParams(vmem_limit_bytes=PACK_VMEM),
        name="pack",
    )(*arrays)


def unpack_kernel(plan, n_in, n_pass, *refs):
    ins, outs = refs[:n_in], refs[n_in + n_pass :]
    for target, (which, row) in zip(outs, plan):
        for m in range(target.shape[1] // (4 * HD)):
            parts = [ins[which][4 * m + n, row : row + HD, :] for n in range(4)]
            target[:, m * 4 * HD : (m + 1) * 4 * HD] = jnp.concatenate(parts, axis=0).T


def unpack(received, half, plan, earlier=()):
    peers, _, tokens = received[0].shape
    columns = 2 * peers * HD
    shape = jax.ShapeDtypeStruct((tokens, columns), jnp.bfloat16)
    n_in, n_pass = len(received), len(earlier)
    return pl.pallas_call(
        functools.partial(unpack_kernel, plan, n_in, n_pass),
        grid=(1,),
        out_shape=(shape,) * len(plan),
        in_specs=[pl.BlockSpec(r.shape, lambda i: (0, 0, 0)) for r in received]
        + [pl.BlockSpec(memory_space=pl.ANY)] * n_pass,
        out_specs=(pl.BlockSpec((tokens, columns // 2), lambda i: (0, half)),) * len(plan),
        input_output_aliases={n_in + n: n for n in range(n_pass)},
        compiler_params=pltpu.CompilerParams(vmem_limit_bytes=32 * 1024 * 1024),
        name="unpack",
    )(*received, *earlier)


def total_kernel(extra, *refs):
    mine, got, out = refs[extra], refs[extra + 1], refs[-1]
    if extra:
        out[:, :HD, :] = refs[0][...]
    base = HD if extra else 0
    out[:, base:, :] = (mine[...] + got[...].astype(jnp.float32)).astype(jnp.bfloat16)


def total(first, mine, got):
    peers, rows, tokens = mine.shape
    extra = len(first)
    steps = 2

    def part(height):
        return pl.BlockSpec((peers // steps, height, tokens), lambda i: (i, 0, 0))

    return pl.pallas_call(
        functools.partial(total_kernel, extra),
        grid=(steps,),
        out_shape=jax.ShapeDtypeStruct((peers, rows + HD * extra, tokens), jnp.bfloat16),
        in_specs=[part(HD)] * extra + [part(rows)] * 2,
        out_specs=part(rows + HD * extra),
        compiler_params=pltpu.CompilerParams(vmem_limit_bytes=TOTAL_VMEM),
        name="total",
    )(*first, mine, got)


def shards(queries, keys_in, values, out_grad, doc_lengths):
    blocks, group = lax.axis_size("blk"), lax.axis_size("head") // 2
    tokens = queries.shape[0]
    devices = 2 * blocks * group
    halves = [list(range(group)), list(range(group, 2 * group))]
    up = [(i, i + group) for i in range(devices - group)]
    down = [(i + group, i) for i in range(devices - group)]

    def exchange(x):
        return lax.all_to_all(
            x, "head", split_axis=0, concat_axis=0, tiled=True, axis_index_groups=halves
        )

    def shift(x, route):
        return lax.ppermute(x, ("blk", "head"), route)

    def after(x, *earlier):
        return lax.optimization_barrier((x, *earlier))[0]

    half_index = lax.axis_index("blk") * 2 + lax.axis_index("head") // group
    base = (half_index * (group * tokens)).astype(jnp.int32).reshape(1)
    pair = ((0, 0), (0, HD))

    def pack_pair(first, second, half):
        return pack((first, second), half, pair, (2 * HD,))[0]

    send_kv_a = pack_pair(keys_in, values, 0)
    send_q_a = pack_pair(queries, out_grad, 0)
    send_kv_b = pack_pair(keys_in, values, 1)
    send_q_b = pack_pair(queries, out_grad, 1)

    own_a = exchange(send_kv_a)
    halo_a = shift(own_a, up)
    rows_a = exchange(after(send_q_a, own_a, send_kv_b, send_q_b))
    own_b = exchange(after(send_kv_b, rows_a, halo_a))
    halo_b = shift(own_b, up)
    send_q_b, dq_a, back_a, mine_a = attend(
        doc_lengths, base, halo_a, own_a, rows_a, 0, CQ, CK, False, (send_q_b,)
    )
    got_a = shift(back_a, down)
    rows_b = exchange(after(send_q_b, own_b))
    sum_a = total((dq_a,), mine_a, got_a)
    out_a = exchange(after(sum_a, rows_b, halo_b))
    dq_b, back_b, mine_b = attend(doc_lengths, base, halo_b, own_b, rows_b, 0, CQ, CK, False)
    got_b = shift(back_b, down)
    out_q = exchange(after(dq_b, out_a))
    sum_b = total((), mine_b, got_b)
    out_b = exchange(after(sum_b, out_q))
    grad_q, grad_k, grad_v = unpack((out_a,), 0, ((0, 0), (0, HD), (0, 2 * HD)))
    (grad_q,) = unpack((out_q,), 1, ((0, 0),), (grad_q,))
    grad_k, grad_v = unpack((out_b,), 1, pair, (grad_k, grad_v))
    return grad_q, grad_k, grad_v


def solution(mesh):
    rows = P(("blk", "head"), None)
    return jax.shard_map(
        shards,
        mesh=mesh,
        in_specs=(rows, rows, rows, rows, P()),
        out_specs=(rows, rows, rows),
        check_vma=False,
    )
```

time: 224 us -> 211 us (0.942)
  the two profiles are of different devices: /device:TPU:5 before, /device:TPU:17 now
where the time goes in v2:
time: 211 us; the launch traced here: 208 us
  waiting for transfers between devices  90.5 us (43%)
  Pallas kernels  58.4 us (28%)
  starting transfers between devices  52 us (25%)
  local copies, waits for them, and re-layouts  6.68 us (3%)
    ppermute x4, waiting for transfers between devices, shift(): return lax.ppermute(x, ('blk', 'head'), route)  46 us
    all_to_all x7, waiting for transfers between devices, exchange(): lax.all_to_all(x, 'head', split_axis=0, concat_axis=0, tiled=True, axis_i...  44.5 us
    all_to_all x7, starting transfers between devices, exchange(): lax.all_to_all(x, 'head', split_axis=0, concat_axis=0, tiled=True, axis_i...  41.7 us
    pallas_call x2, Pallas kernels, attend(): pl.pallas_call(functools.partial(attend_kernel, spec), grid=(nc // cq,),...  39.4 us
    pallas_call x4, Pallas kernels, pack(): pl.pallas_call(functools.partial(pack_kernel, plan), grid=(steps,), out_s...  13.9 us
    ppermute x4, starting transfers between devices, shift(): return lax.ppermute(x, ('blk', 'head'), route)  10.3 us
    unnamed x16, local copies, waits for them, and re-layouts  6.68 us
  transfers between devices with their start and end apart: 11, of which 9 were waited for; matrix products, arithmetic and copies ran while one was open for 0% of the time, Pallas kernels for 26%

profile of v2, /device:TPU:17, one launch (start us, length us, event | category | flops | bytes accessed | tf_op | source)
XLA Modules:
  0.0 208.3 jit_solution(3496947395794468410)
XLA Ops:
  0.6 3.5 %pack.6 = bf16[16,192,128]{2,1,0:T(8,128)(2,1)} custom-call(bf16[128,3072]{1,0:T(8,128)(2,1)} %refs_0_.6, bf16[128,3072]{1,0:T(8,128)(2,1)} %refs_1_.6), custom_call_target="tpu_custom_call" | custom-call | tf_op jit(solution)/shard_map/pack/pallas_call | solution.py:257
  4.1 9.2 %all-to-all-start = ((bf16[16,192,128]{2,1,0:T(8,128)(2,1)}), bf16[16,192,128]{2,1,0:T(8,128)(2,1)S(1)}, u32[]{:S(2)}, u32[]{:S(2)}) async-start(bf16[16,192,128]{2,1,0:T(8,128)(2,1)} %pack.6), calls=%async_computation | async-start | bytes 1572864 | tf_op jit(solution)/shard_map/all_to_all | solution.py:330
  13.3 3.5 %pack.4 = bf16[16,192,128]{2,1,0:T(8,128)(2,1)} custom-call(bf16[128,3072]{1,0:T(8,128)(2,1)} %refs_0_.6, bf16[128,3072]{1,0:T(8,128)(2,1)} %refs_1_.6), custom_call_target="tpu_custom_call" | custom-call | tf_op jit(solution)/shard_map/pack/pallas_call | solution.py:257
  16.7 3.4 %pack.7.refs_0_ = bf16[16,192,128]{2,1,0:T(8,128)(2,1)} custom-call(bf16[128,3072]{1,0:T(8,128)(2,1)} %refs_0_.7, bf16[128,3072]{1,0:T(8,128)(2,1)} %refs_1_.7), custom_call_target="tpu_custom_call" | custom-call | tf_op jit(solution)/shard_map/pack/pallas_call | solution.py:257
  20.2 3.5 %pack.5 = bf16[16,192,128]{2,1,0:T(8,128)(2,1)} custom-call(bf16[128,3072]{1,0:T(8,128)(2,1)} %refs_0_.7, bf16[128,3072]{1,0:T(8,128)(2,1)} %refs_1_.7), custom_call_target="tpu_custom_call" | custom-call | tf_op jit(solution)/shard_map/pack/pallas_call | solution.py:257
  23.7 12.3 %all-to-all-done.own = bf16[16,192,128]{2,1,0:T(8,128)(2,1)S(1)} async-done(((bf16[16,192,128]{2,1,0:T(8,128)(2,1)}), bf16[16,192,128]{2,1,0:T(8,128)(2,1)S(1)}, u32[]{:S(2)}, u32[]{:S(2)}) %all-to-all-start) | async-done | bytes 786464 | tf_op jit(solution)/shard_map/all_to_all | solution.py:330
  35.9 3.5 %all-to-all-start.1 = ((bf16[16,192,128]{2,1,0:T(8,128)(2,1)}), bf16[16,192,128]{2,1,0:T(8,128)(2,1)S(1)}, u32[]{:S(2)}, u32[]{:S(2)}) async-start(bf16[16,192,128]{2,1,0:T(8,128)(2,1)} %pack.5), calls=%async_computation.1 | async-start | bytes 1572864 | tf_op jit(solution)/shard_map/all_to_all | solution.py:330
  39.4 3.1 %collective-permute-start = (bf16[16,192,128]{2,1,0:T(8,128)(2,1)S(1)}, bf16[16,192,128]{2,1,0:T(8,128)(2,1)S(1)}, u32[]{:S(2)}, u32[]{:S(2)}) collective-permute-start(bf16[16,192,128]{2,1,0:T(8,128)(2,1)S(1)} %all-to-all-done.own), channel_id=1, source_target_pairs={{0,16},{1,17},{2,18},{3,19},{4,20},{5,21},{6,22},{7,23},{8,24},{9,... | collective-permute-start | bytes 2359304 | tf_op jit(solution)/shard_map/ppermute | solution.py:335
  42.6 20.2 %collective-permute-done.halo = bf16[16,192,128]{2,1,0:T(8,128)(2,1)S(1)} collective-permute-done((bf16[16,192,128]{2,1,0:T(8,128)(2,1)S(1)}, bf16[16,192,128]{2,1,0:T(8,128)(2,1)S(1)}, u32[]{:S(2)}, u32[]{:S(2)}) %collective-permute-start) | collective-permute-done | bytes 786464 | tf_op jit(solution)/shard_map/ppermute | solution.py:335
  62.8 7.1 %all-to-all-start.2 = ((bf16[16,192,128]{2,1,0:T(8,128)(2,1)}), bf16[16,192,128]{2,1,0:T(8,128)(2,1)S(1)}, u32[]{:S(2)}, u32[]{:S(2)}) async-start(bf16[16,192,128]{2,1,0:T(8,128)(2,1)} %pack.4), calls=%async_computation.2 | async-start | bytes 1572864 | tf_op jit(solution)/shard_map/all_to_all | solution.py:330
  69.9 19.7 %attend.2 = (bf16[16,192,128]{2,1,0:T(8,128)(2,1)}, bf16[16,96,128]{2,1,0:T(8,128)(2,1)S(1)}, bf16[16,192,128]{2,1,0:T(8,128)(2,1)}, f32[16,192,128]{2,1,0:T(8,128)S(1)}) custom-call(s32[32]{0:T(128)S(1)} %copy-done.7, s32[1]{0:T(128)} %bitcast.base, bf16[16,192,128]{2,1,0:T(8,128)(2,1)S(1)} %collective-permute-done.halo, ...), custom_call_target="tpu_custom_call", output_to_operand_aliasing={{0}: (5, {})} | custom-call | tf_op jit(solution)/shard_map/attend/pallas_call | solution.py:213
  89.6 1.2 copy-done.2
  92.6 6.4 %all-to-all-start.3 = ((bf16[16,192,128]{2,1,0:T(8,128)(2,1)}), bf16[16,192,128]{2,1,0:T(8,128)(2,1)S(1)}, u32[]{:S(2)}, u32[]{:S(2)}) async-start(bf16[16,192,128]{2,1,0:T(8,128)(2,1)} %get-tuple-element.24), calls=%async_computation.3 | async-start | bytes 1572864 | tf_op jit(solution)/shard_map/all_to_all | solution.py:330
  98.9 1.9 collective-permute-start.2
  100.9 3.4 %collective-permute-start.1 = (bf16[16,192,128]{2,1,0:T(8,128)(2,1)S(1)}, bf16[16,192,128]{2,1,0:T(8,128)(2,1)S(1)}, u32[]{:S(2)}, u32[]{:S(2)}) collective-permute-start(bf16[16,192,128]{2,1,0:T(8,128)(2,1)S(1)} %all-to-all-done.2.own), channel_id=1, source_target_pairs={{0,16},{1,17},{2,18},{3,19},{4,20},{5,21},{6,22},{7,23},{8,24},{9,... | collective-permute-start | bytes 2359304 | tf_op jit(solution)/shard_map/ppermute | solution.py:335
  104.3 15.9 %collective-permute-done.2.refs_2_ = bf16[16,192,128]{2,1,0:T(8,128)(2,1)S(1)} collective-permute-done((bf16[16,192,128]{2,1,0:T(8,128)(2,1)}, bf16[16,192,128]{2,1,0:T(8,128)(2,1)S(1)}, u32[]{:S(2)}, u32[]{:S(2)}) %collective-permute-start.2) | collective-permute-done | bytes 786464 | tf_op jit(solution)/shard_map/ppermute | solution.py:335
  120.1 1.4 copy-done.3
  121.6 1.1 total.2
  122.7 1.3 collective-permute-done.1.halo
  124.0 7.7 %all-to-all-start.4 = ((bf16[16,288,128]{2,1,0:T(8,128)(2,1)}), bf16[16,288,128]{2,1,0:T(8,128)(2,1)S(1)}, u32[]{:S(2)}, u32[]{:S(2)}) async-start(bf16[16,288,128]{2,1,0:T(8,128)(2,1)} %total.2), calls=%async_computation.4 | async-start | bytes 2359296 | tf_op jit(solution)/shard_map/all_to_all | solution.py:330
  131.7 19.7 %attend.3 = (bf16[16,96,128]{2,1,0:T(8,128)(2,1)S(1)}, bf16[16,192,128]{2,1,0:T(8,128)(2,1)}, f32[16,192,128]{2,1,0:T(8,128)S(1)}) custom-call(s32[32]{0:T(128)S(1)} %copy-done.7, s32[1]{0:T(128)} %bitcast.base, bf16[16,192,128]{2,1,0:T(8,128)(2,1)S(1)} %collective-permute-done.1.halo, bf16[16,192,128]{2,1,0:T(8,128)(2,1)S(1)} %all-to-all-done.2.own, ...), custom_call_target="tpu_custom_call" | custom-call | tf_op jit(solution)/shard_map/attend/pallas_call | solution.py:213
  151.4 1.2 copy-done
  153.3 1.9 collective-permute-start.3
  155.2 7.0 %all-to-all-done.4.refs_0_ = bf16[16,288,128]{2,1,0:T(8,128)(2,1)S(1)} async-done(((bf16[16,288,128]{2,1,0:T(8,128)(2,1)}), bf16[16,288,128]{2,1,0:T(8,128)(2,1)S(1)}, u32[]{:S(2)}, u32[]{:S(2)}) %all-to-all-start.4) | async-done | bytes 1179680 | tf_op jit(solution)/shard_map/all_to_all | solution.py:330
  162.2 3.7 %all-to-all-start.5 = ((bf16[16,96,128]{2,1,0:T(8,128)(2,1)}), bf16[16,96,128]{2,1,0:T(8,128)(2,1)S(1)}, u32[]{:S(2)}, u32[]{:S(2)}) async-start(bf16[16,96,128]{2,1,0:T(8,128)(2,1)} %copy-done.4), calls=%async_computation.5 | async-start | bytes 786432 | tf_op jit(solution)/shard_map/all_to_all | solution.py:330
  165.9 8.6 %collective-permute-done.3.refs_1_ = bf16[16,192,128]{2,1,0:T(8,128)(2,1)S(1)} collective-permute-done((bf16[16,192,128]{2,1,0:T(8,128)(2,1)}, bf16[16,192,128]{2,1,0:T(8,128)(2,1)S(1)}, u32[]{:S(2)}, u32[]{:S(2)}) %collective-permute-start.3) | collective-permute-done | bytes 786464 | tf_op jit(solution)/shard_map/ppermute | solution.py:335
  174.5 1.4 copy-done.1
  176.9 3.6 %all-to-all-done.5.refs_0_ = bf16[16,96,128]{2,1,0:T(8,128)(2,1)S(1)} async-done(((bf16[16,96,128]{2,1,0:T(8,128)(2,1)}), bf16[16,96,128]{2,1,0:T(8,128)(2,1)S(1)}, u32[]{:S(2)}, u32[]{:S(2)}) %all-to-all-start.5) | async-done | bytes 393248 | tf_op jit(solution)/shard_map/all_to_all | solution.py:330
  180.5 4.1 %all-to-all-start.6 = ((bf16[16,192,128]{2,1,0:T(8,128)(2,1)}), bf16[16,192,128]{2,1,0:T(8,128)(2,1)S(1)}, u32[]{:S(2)}, u32[]{:S(2)}) async-start(bf16[16,192,128]{2,1,0:T(8,128)(2,1)} %total.3), calls=%async_computation.6 | async-start | bytes 1572864 | tf_op jit(solution)/shard_map/all_to_all | solution.py:330
  184.6 1.2 unpack.3
  186.7 20.6 %all-to-all-done.6.refs_0_ = bf16[16,192,128]{2,1,0:T(8,128)(2,1)S(1)} async-done(((bf16[16,192,128]{2,1,0:T(8,128)(2,1)}), bf16[16,192,128]{2,1,0:T(8,128)(2,1)S(1)}, u32[]{:S(2)}, u32[]{:S(2)}) %all-to-all-start.6) | async-done | bytes 786464 | tf_op jit(solution)/shard_map/all_to_all | solution.py:330
  207.3 1.0 unpack.5
  (17 shorter events, 4.4 us)
Async XLA Ops:
  4.1 31.8 %all-to-all-start = ((bf16[16,192,128]{2,1,0:T(8,128)(2,1)}), bf16[16,192,128]{2,1,0:T(8,128)(2,1)S(1)}, u32[]{:S(2)}, u32[]{:S(2)}) async-start(bf16[16,192,128]{2,1,0:T(8,128)(2,1)} %pack.6), calls=%async_computation | async-start | bytes 1572864 | tf_op jit(solution)/shard_map/all_to_all | solution.py:330
  23.7 46.3 %copy-start.7 = (s32[32]{0:T(128)S(1)}, s32[32]{0:T(128)}, u32[]{:S(2)}) copy-start(s32[32]{0:T(128)} %lens.3) | copy-start | bytes 388
  35.9 26.9 %all-to-all-start.1 = ((bf16[16,192,128]{2,1,0:T(8,128)(2,1)}), bf16[16,192,128]{2,1,0:T(8,128)(2,1)S(1)}, u32[]{:S(2)}, u32[]{:S(2)}) async-start(bf16[16,192,128]{2,1,0:T(8,128)(2,1)} %pack.5), calls=%async_computation.1 | async-start | bytes 1572864 | tf_op jit(solution)/shard_map/all_to_all | solution.py:330
  39.4 23.3 %collective-permute-start = (bf16[16,192,128]{2,1,0:T(8,128)(2,1)S(1)}, bf16[16,192,128]{2,1,0:T(8,128)(2,1)S(1)}, u32[]{:S(2)}, u32[]{:S(2)}) collective-permute-start(bf16[16,192,128]{2,1,0:T(8,128)(2,1)S(1)} %all-to-all-done.own), channel_id=1, source_target_pairs={{0,16},{1,17},{2,18},{3,19},{4,20},{5,21},{6,22},{7,23},{8,24},{9,... | collective-permute-start | bytes 2359304 | tf_op jit(solution)/shard_map/ppermute | solution.py:335
  62.8 29.8 %all-to-all-start.2 = ((bf16[16,192,128]{2,1,0:T(8,128)(2,1)}), bf16[16,192,128]{2,1,0:T(8,128)(2,1)S(1)}, u32[]{:S(2)}, u32[]{:S(2)}) async-start(bf16[16,192,128]{2,1,0:T(8,128)(2,1)} %pack.4), calls=%async_computation.2 | async-start | bytes 1572864 | tf_op jit(solution)/shard_map/all_to_all | solution.py:330
  89.6 1.2 copy-start.2
  90.8 0.7 copy-start.5
  92.6 27.6 %copy-start.6 = (bf16[16,96,128]{2,1,0:T(8,128)(2,1)S(1)}, bf16[16,96,128]{2,1,0:T(8,128)(2,1)}, u32[]{:S(2)}) copy-start(bf16[16,96,128]{2,1,0:T(8,128)(2,1)} %copy-done.5) | copy-start | bytes 1179652
  92.6 31.4 %all-to-all-start.3 = ((bf16[16,192,128]{2,1,0:T(8,128)(2,1)}), bf16[16,192,128]{2,1,0:T(8,128)(2,1)S(1)}, u32[]{:S(2)}, u32[]{:S(2)}) async-start(bf16[16,192,128]{2,1,0:T(8,128)(2,1)} %get-tuple-element.24), calls=%async_computation.3 | async-start | bytes 1572864 | tf_op jit(solution)/shard_map/all_to_all | solution.py:330
  98.9 21.2 %collective-permute-start.2 = (bf16[16,192,128]{2,1,0:T(8,128)(2,1)}, bf16[16,192,128]{2,1,0:T(8,128)(2,1)S(1)}, u32[]{:S(2)}, u32[]{:S(2)}) collective-permute-start(bf16[16,192,128]{2,1,0:T(8,128)(2,1)} %get-tuple-element.28), channel_id=1, source_target_pairs={{16,0},{17,1},{18,2},{19,3},{20,4},{21,5},{22,6},{23,7},{24,8},{25... | collective-permute-start | bytes 2359304 | tf_op jit(solution)/shard_map/ppermute | solution.py:335
  100.9 23.1 %collective-permute-start.1 = (bf16[16,192,128]{2,1,0:T(8,128)(2,1)S(1)}, bf16[16,192,128]{2,1,0:T(8,128)(2,1)S(1)}, u32[]{:S(2)}, u32[]{:S(2)}) collective-permute-start(bf16[16,192,128]{2,1,0:T(8,128)(2,1)S(1)} %all-to-all-done.2.own), channel_id=1, source_target_pairs={{0,16},{1,17},{2,18},{3,19},{4,20},{5,21},{6,22},{7,23},{8,24},{9,... | collective-permute-start | bytes 2359304 | tf_op jit(solution)/shard_map/ppermute | solution.py:335
  120.1 1.4 copy-start.3
  124.0 38.3 %all-to-all-start.4 = ((bf16[16,288,128]{2,1,0:T(8,128)(2,1)}), bf16[16,288,128]{2,1,0:T(8,128)(2,1)S(1)}, u32[]{:S(2)}, u32[]{:S(2)}) async-start(bf16[16,288,128]{2,1,0:T(8,128)(2,1)} %total.2), calls=%async_computation.4 | async-start | bytes 2359296 | tf_op jit(solution)/shard_map/all_to_all | solution.py:330
  151.4 1.2 copy-start
  152.6 0.7 copy-start.4
  153.3 21.2 %collective-permute-start.3 = (bf16[16,192,128]{2,1,0:T(8,128)(2,1)}, bf16[16,192,128]{2,1,0:T(8,128)(2,1)S(1)}, u32[]{:S(2)}, u32[]{:S(2)}) collective-permute-start(bf16[16,192,128]{2,1,0:T(8,128)(2,1)} %get-tuple-element.33), channel_id=1, source_target_pairs={{16,0},{17,1},{18,2},{19,3},{20,4},{21,5},{22,6},{23,7},{24,8},{25... | collective-permute-start | bytes 2359304 | tf_op jit(solution)/shard_map/ppermute | solution.py:335
  162.2 18.3 %all-to-all-start.5 = ((bf16[16,96,128]{2,1,0:T(8,128)(2,1)}), bf16[16,96,128]{2,1,0:T(8,128)(2,1)S(1)}, u32[]{:S(2)}, u32[]{:S(2)}) async-start(bf16[16,96,128]{2,1,0:T(8,128)(2,1)} %copy-done.4), calls=%async_computation.5 | async-start | bytes 786432 | tf_op jit(solution)/shard_map/all_to_all | solution.py:330
  174.5 1.4 copy-start.1
  180.5 26.8 %all-to-all-start.6 = ((bf16[16,192,128]{2,1,0:T(8,128)(2,1)}), bf16[16,192,128]{2,1,0:T(8,128)(2,1)S(1)}, u32[]{:S(2)}, u32[]{:S(2)}) async-start(bf16[16,192,128]{2,1,0:T(8,128)(2,1)} %total.3), calls=%async_computation.6 | async-start | bytes 1572864 | tf_op jit(solution)/shard_map/all_to_all | solution.py:330

commit v3 on v2

--- a/solution.py
+++ b/solution.py
@@ -8,12 +8,9 @@
 
 HD = 96
 CH = 128
-CQ = 4
-CK = 2
 PACK_VMEM = 56 * 1024 * 1024
-TOTAL_VMEM = 16 * 1024 * 1024
+TOTAL_VMEM = 56 * 1024 * 1024
 SUB = 2
-RUNS = (4, 2, 1)
 ATTEND_VMEM = 40 * 1024 * 1024
 FACTOR = 1.0 / math.sqrt(HD)
 LOG2 = FACTOR * math.log2(math.e)
@@ -22,7 +19,7 @@
 def attend_kernel(spec, lens, base, halo, own, qd, *refs):
     dq, back, mine = refs[-10:-7]
     (kvt, kn, vn, score, acc, oacc, qacc) = refs[-7:]
-    nc, docs, cq, ck, q_row, native = spec
+    nc, docs, cq, ck, q_row = spec
     tq, tk = cq * CH, ck * CH
     span = nc * CH
     first = base[0]
@@ -75,13 +72,12 @@
     def q_step(i):
         q_chunk = i * cq
         q_begin = span + i * tq
-        begin, lo, hi = jnp.int32(0), jnp.int32(0), jnp.int32(0)
+        begin, lo = jnp.int32(0), jnp.int32(0)
         q_pos = q_begin + lax.broadcasted_iota(jnp.int32, (1, tq), 1)
         start_row = jnp.zeros((1, tq), jnp.int32)
         for d in range(docs):
             here = begin - origin
             lo = jnp.where(here <= q_begin, here, lo)
-            hi = jnp.where(here <= q_begin + (tq - 1), here, hi)
             start_row = jnp.where(q_pos >= here, here, start_row)
             begin = begin + lens[d]
         k_first = lo // tk
@@ -89,143 +85,147 @@
         qt = wide(qd, q_chunk, pl.ds(q_row, HD), cq)
         gt = wide(qd, q_chunk, pl.ds(q_row + HD, HD), cq)
 
-        def rows_of(j, n):
-            return pl.ds(pl.multiple_of(j * tk + n * CH * SUB, CH * SUB), CH * SUB)
-
-        def slot_of(j, n):
-            return pl.ds(pl.multiple_of((j - k_first) * tk + n * CH * SUB, CH * SUB), CH * SUB)
-
-        size = CH * SUB
-
-        def sweep(step, carry):
-            j = k_first
-            for run in RUNS:
-                count = (k_last - j) // run
-                parts = run * ck // SUB
-                carry = lax.fori_loop(0, count, lambda t, c: step(j + t * run, parts, c), carry)
-                j = j + count * run
-            return carry
-
-        def score_step(j, parts, top):
-            def product(n):
-                return jnp.dot(kn[rows_of(j, n), :], qt, preferred_element_type=jnp.float32)
-
-            s = product(0)
-            for n in range(parts):
-                later = product(n + 1) if n + 1 < parts else None
-                k_pos = j * tk + n * size + lax.broadcasted_iota(jnp.int32, (size, tq), 0)
-                s = jnp.where((k_pos >= start_row) & (k_pos <= q_pos), s, -1e30)
-                score[slot_of(j, n), :] = s
-                top = jnp.maximum(top, jnp.max(s.reshape(size // 8, 8, tq), axis=0))
-                s = later
-            return top
-
-        top = sweep(score_step, jnp.full((8, tq), -1e30, jnp.float32))
-        top = jnp.max(top, axis=0, keepdims=True)
-        oacc[...] = jnp.zeros_like(oacc)
-
-        def power_step(j, parts, total):
-            out, held = None, None
-            for n in range(parts + 1):
-                if n < parts:
-                    p = jnp.exp2((score[slot_of(j, n), :] - top) * LOG2)
-                    score[slot_of(j, n), :] = p
-                    total = total + jnp.sum(p.reshape(size // 8, 8, tq), axis=0)
-                    narrow = p.astype(jnp.bfloat16)
-                if n:
-                    vt = wide(kvt, j * ck + (n - 1) * SUB, pl.ds(HD, HD), SUB)
-                    term = jnp.dot(vt, held, preferred_element_type=jnp.float32)
-                    out = term if out is None else out + term
-                held = narrow
-            oacc[...] += out
-            return total
-
-        total = sweep(power_step, jnp.zeros((8, tq), jnp.float32))
-        inverse = 1.0 / jnp.sum(total, axis=0, keepdims=True)
-        attended = (oacc[...] * inverse).astype(jnp.bfloat16).astype(jnp.float32)
-        delta = jnp.sum(gt.astype(jnp.float32) * attended, axis=0, keepdims=True)
-        qacc[...] = jnp.zeros_like(qacc)
-
-        def grad_step(j, parts, _):
-            last = (((1,), (1,)), ((), ()))
-
-            def product(n):
-                return jnp.dot(vn[rows_of(j, n), :], gt, preferred_element_type=jnp.float32)
-
-            prob, held, out = product(0), None, None
-            for n in range(parts + 1):
-                later = product(n + 1) if n + 1 < parts else None
-                if n < parts:
-                    shares = score[slot_of(j, n), :] * inverse
-                    weights = shares.astype(jnp.bfloat16)
-                    grad = (shares * (prob - delta)).astype(jnp.bfloat16)
-                if n:
-                    old_weights, old_grad = held
-                    m = j * ck + (n - 1) * SUB
-                    kt = wide(kvt, m, pl.ds(0, HD), SUB)
-                    term = jnp.dot(kt, old_grad, preferred_element_type=jnp.float32)
-                    out = term if out is None else out + term
-                    dk = lax.dot_general(qt, old_grad, last, preferred_element_type=jnp.float32)
-                    dv = lax.dot_general(gt, old_weights, last, preferred_element_type=jnp.float32)
-                    for c in range(SUB):
-                        cols = slice(c * CH, (c + 1) * CH)
-                        acc[m + c, :HD, :] += dk[:, cols]
-                        acc[m + c, HD:, :] += dv[:, cols]
-                held = (weights, grad)
-                prob = later
-            qacc[...] += out
-            return 0
-
-        sweep(grad_step, 0)
-        out = (qacc[...] * FACTOR).astype(jnp.bfloat16)
-        for n in range(cq):
-            dq[n] = out[:, n * CH : (n + 1) * CH]
-            done = acc[i * cq + n]
-            back[n, :HD, :] = (done[:HD] * FACTOR).astype(jnp.bfloat16)
-            back[n, HD:, :] = done[HD:].astype(jnp.bfloat16)
-
-    q_step(step)
+        def run(count):
+            def rows_of(j, n):
+                return pl.ds(pl.multiple_of(j * tk + n * CH * SUB, CH * SUB), CH * SUB)
+
+            def slot_of(j, n):
+                return pl.ds(n * CH * SUB, CH * SUB)
+
+            size = CH * SUB
+
+            def sweep(step, carry):
+                return step(k_first, count * ck // SUB, carry)
+
+            def score_step(j, parts, top):
+                def product(n):
+                    return jnp.dot(kn[rows_of(j, n), :], qt, preferred_element_type=jnp.float32)
+
+                s = product(0)
+                for n in range(parts):
+                    later = product(n + 1) if n + 1 < parts else None
+                    k_pos = j * tk + n * size + lax.broadcasted_iota(jnp.int32, (size, tq), 0)
+                    keep = k_pos >= start_row
+                    if (n + 1) * size > count * tk - tq:
+                        keep = keep & (k_pos <= q_pos)
+                    s = jnp.where(keep, s, -1e30)
+                    score[slot_of(j, n), :] = s
+                    top = jnp.maximum(top, jnp.max(s.reshape(size // 8, 8, tq), axis=0))
+                    s = later
+                return top
+
+            top = sweep(score_step, jnp.full((8, tq), -1e30, jnp.float32))
+            top = jnp.max(top, axis=0, keepdims=True)
+            oacc[...] = jnp.zeros_like(oacc)
+
+            def power_step(j, parts, total):
+                out, held = None, None
+                for n in range(parts + 1):
+                    if n < parts:
+                        p = jnp.exp2((score[slot_of(j, n), :] - top) * LOG2)
+                        score[slot_of(j, n), :] = p
+                        total = total + jnp.sum(p.reshape(size // 8, 8, tq), axis=0)
+                        narrow = p.astype(jnp.bfloat16)
+                    if n:
+                        vt = wide(kvt, j * ck + (n - 1) * SUB, pl.ds(HD, HD), SUB)
+                        term = jnp.dot(vt, held, preferred_element_type=jnp.float32)
+                        out = term if out is None else out + term
+                    held = narrow
+                oacc[...] += out
+                return total
+
+            total = sweep(power_step, jnp.zeros((8, tq), jnp.float32))
+            inverse = 1.0 / jnp.sum(total, axis=0, keepdims=True)
+            attended = (oacc[...] * inverse).astype(jnp.bfloat16).astype(jnp.float32)
+            delta = jnp.sum(gt.astype(jnp.float32) * attended, axis=0, keepdims=True)
+            qacc[...] = jnp.zeros_like(qacc)
+
+            def grad_step(j, parts, _):
+                last = (((1,), (1,)), ((), ()))
+
+                def product(n):
+                    return jnp.dot(vn[rows_of(j, n), :], gt, preferred_element_type=jnp.float32)
+
+                prob, held, out = product(0), None, None
+                for n in range(parts + 1):
+                    later = product(n + 1) if n + 1 < parts else None
+                    if n < parts:
+                        shares = score[slot_of(j, n), :] * inverse
+                        weights = shares.astype(jnp.bfloat16)
+                        grad = (shares * (prob - delta)).astype(jnp.bfloat16)
+                    if n:
+                        old_weights, old_grad = held
+                        m = j * ck + (n - 1) * SUB
+                        kt = wide(kvt, m, pl.ds(0, HD), SUB)
+                        term = jnp.dot(kt, old_grad, preferred_element_type=jnp.float32)
+                        out = term if out is None else out + term
+                        dk = lax.dot_general(qt, old_grad, last, preferred_element_type=jnp.float32)
+                        dv = lax.dot_general(gt, old_weights, last, preferred_element_type=jnp.float32)
+                        for c in range(SUB):
+                            cols = slice(c * CH, (c + 1) * CH)
+                            acc[m + c, :HD, :] += dk[:, cols]
+                            acc[m + c, HD:, :] += dv[:, cols]
+                    held = (weights, grad)
+                    prob = later
+                qacc[...] += out
+                return 0
+
+            sweep(grad_step, 0)
+            out = (qacc[...] * FACTOR).astype(jnp.bfloat16)
+            for n in range(cq):
+                dq[n] = out[:, n * CH : (n + 1) * CH]
+                done = acc[nc + i * cq + n]
+                mine[n, :HD, :] = done[:HD] * FACTOR
+                mine[n, HD:, :] = done[HD:]
+
+        for count in range(1, (nc * CH + tq - 1) // tk + 2):
+            pl.when(k_last - k_first == count)(functools.partial(run, count))
+
+    q_step(nc // cq - 1 - step)
 
     @pl.when(step == nc // cq - 1)
     def _():
         def finish(c, _):
-            mine[c, :HD, :] = acc[nc + c, :HD, :] * FACTOR
-            mine[c, HD:, :] = acc[nc + c, HD:, :]
+            back[c, :HD, :] = (acc[c, :HD, :] * FACTOR).astype(jnp.bfloat16)
+            back[c, HD:, :] = acc[c, HD:, :].astype(jnp.bfloat16)
             return 0
 
         lax.fori_loop(0, nc, finish, 0, unroll=2)
 
 
-def attend(lens, base, halo, own, qd, q_row, cq=2, ck=2, native=True, carried=()):
+def attend(lens, base, halo, own, qd, q_row, into=None, cq=2, ck=2):
     nc = halo.shape[0]
     tq, tk = cq * CH, ck * CH
     window = nc * CH + tq + tk
-    spec = (nc, lens.shape[0], cq, ck, q_row, native)
+    spec = (nc, lens.shape[0], cq, ck, q_row)
     smem = pl.BlockSpec(memory_space=pltpu.SMEM)
+
+    steps = nc // cq
 
     def whole(x):
         return pl.BlockSpec(x.shape, lambda i: (0, 0, 0))
 
     def part(rows):
-        return pl.BlockSpec((cq, rows, CH), lambda i: (i, 0, 0))
-
-    through = [pl.BlockSpec(memory_space=pl.ANY)] * len(carried)
+        return pl.BlockSpec((cq, rows, CH), lambda i: (steps - 1 - i, 0, 0))
+
+    through, extra, target, slot = [], (), (nc, HD, CH), 0
+    if into is not None:
+        through, extra, target = [pl.BlockSpec(memory_space=pl.ANY)], (into,), into.shape
+        slot = into.shape[1] // HD - 1
     return pl.pallas_call(
         functools.partial(attend_kernel, spec),
         grid=(nc // cq,),
-        out_shape=tuple(jax.ShapeDtypeStruct(x.shape, x.dtype) for x in carried)
-        + (
-            jax.ShapeDtypeStruct((nc, HD, CH), jnp.bfloat16),
+        out_shape=(
+            pltpu.HBM(target, jnp.bfloat16),
             jax.ShapeDtypeStruct((nc, 2 * HD, CH), jnp.bfloat16),
-            jax.ShapeDtypeStruct((nc, 2 * HD, CH), jnp.float32),
+            pltpu.HBM((nc, 2 * HD, CH), jnp.float32),
         ),
         in_specs=[smem, smem, whole(halo), whole(own), whole(qd)] + through,
-        input_output_aliases={5 + n: n for n in range(len(carried))},
-        out_specs=tuple(through)
-        + (
-            part(HD),
+        input_output_aliases={5: 0} if extra else {},
+        out_specs=(
+            pl.BlockSpec((cq, HD, CH), lambda i: (steps - 1 - i, slot, 0)),
+            pl.BlockSpec((nc, 2 * HD, CH), lambda i: (0, 0, 0)),
             part(2 * HD),
-            pl.BlockSpec((nc, 2 * HD, CH), lambda i: (0, 0, 0)),
         ),
         scratch_shapes=[
             pltpu.VMEM((2 * nc, 2 * HD, CH), jnp.bfloat16),
@@ -238,7 +238,7 @@
         ],
         compiler_params=pltpu.CompilerParams(vmem_limit_bytes=ATTEND_VMEM),
         name="attend",
-    )(lens, base, halo, own, qd, *carried)
+    )(lens, base, halo, own, qd, *extra)
 
 
 def pack_kernel(plan, *refs):
@@ -354,14 +354,12 @@
     rows_a = exchange(after(send_q_a, own_a, send_kv_b, send_q_b))
     own_b = exchange(after(send_kv_b, rows_a, halo_a))
     halo_b = shift(own_b, up)
-    send_q_b, dq_a, back_a, mine_a = attend(
-        doc_lengths, base, halo_a, own_a, rows_a, 0, CQ, CK, False, (send_q_b,)
-    )
+    dq_a, back_a, mine_a = attend(doc_lengths, base, halo_a, own_a, rows_a, 0)
     got_a = shift(back_a, down)
-    rows_b = exchange(after(send_q_b, own_b))
+    rows_b = exchange(after(send_q_b, own_b, dq_a))
     sum_a = total((dq_a,), mine_a, got_a)
     out_a = exchange(after(sum_a, rows_b, halo_b))
-    dq_b, back_b, mine_b = attend(doc_lengths, base, halo_b, own_b, rows_b, 0, CQ, CK, False)
+    dq_b, back_b, mine_b = attend(doc_lengths, base, halo_b, own_b, rows_b, 0)
     got_b = shift(back_b, down)
     out_q = exchange(after(dq_b, out_a))
     sum_b = total((), mine_b, got_b)

time: 211 us -> 207 us (0.981)
  Pallas kernels: 58.4 us -> 48.6 us
  waiting for transfers between devices: 90.5 us -> 99.4 us
  local copies, waits for them, and re-layouts: 6.68 us -> 2.64 us
    all_to_all x7, waiting for transfers between devices: 44.5 us -> 59.6 us  [exchange(): lax.all_to_all(x, 'head', split_axis=0, concat_axis=0, tiled=True, axis_i...]
    pallas_call x2, Pallas kernels: 39.4 us -> 26.7 us  [attend(): pl.pallas_call(functools.partial(attend_kernel, spec), grid=(nc // cq,),...]
    ppermute x4, waiting for transfers between devices: 46 us -> 39.8 us  [shift(): return lax.ppermute(x, ('blk', 'head'), route)]
    ppermute x4, starting transfers between devices: 10.3 us -> 14.8 us  [shift(): return lax.ppermute(x, ('blk', 'head'), route)]
    unnamed x16 -> x10, local copies, waits for them, and re-layouts: 6.68 us -> 2.64 us
    all_to_all x7, starting transfers between devices: 41.7 us -> 38 us  [exchange(): lax.all_to_all(x, 'head', split_axis=0, concat_axis=0, tiled=True, axis_i...]
    pallas_call x2, Pallas kernels: 2.07 us -> 5.01 us  [total(): pl.pallas_call(functools.partial(total_kernel, extra), grid=(steps,), out...]
  transfers between devices with their start and end apart: 11 -> 11, of which waited for: 9 -> 9; matrix products, arithmetic and copies ran while one was open for 0% -> 0% of each run, Pallas kernels for 26% -> 22%
where the time goes in v3:
time: 207 us; the launch traced here: 204 us
  waiting for transfers between devices  99.4 us (48%)
  starting transfers between devices  52.8 us (26%)
  Pallas kernels  48.6 us (23%)
  local copies, waits for them, and re-layouts  2.64 us (1%)
    all_to_all x7, waiting for transfers between devices, exchange(): lax.all_to_all(x, 'head', split_axis=0, concat_axis=0, tiled=True, axis_i...  59.6 us
    ppermute x4, waiting for transfers between devices, shift(): return lax.ppermute(x, ('blk', 'head'), route)  39.8 us
    all_to_all x7, starting transfers between devices, exchange(): lax.all_to_all(x, 'head', split_axis=0, concat_axis=0, tiled=True, axis_i...  38 us
    pallas_call x2, Pallas kernels, attend(): pl.pallas_call(functools.partial(attend_kernel, spec), grid=(nc // cq,),...  26.7 us
    ppermute x4, starting transfers between devices, shift(): return lax.ppermute(x, ('blk', 'head'), route)  14.8 us
    pallas_call x4, Pallas kernels, pack(): pl.pallas_call(functools.partial(pack_kernel, plan), grid=(steps,), out_s...  13.9 us
    pallas_call x2, Pallas kernels, total(): pl.pallas_call(functools.partial(total_kernel, extra), grid=(steps,), out...  5.01 us
  transfers between devices with their start and end apart: 11, of which 9 were waited for; matrix products, arithmetic and copies ran while one was open for 0% of the time, Pallas kernels for 22%

profile of v3, /device:TPU:17, one launch (start us, length us, event | category | flops | bytes accessed | tf_op | source)
XLA Modules:
  0.0 204.3 jit_solution(4327088367628892235)
XLA Ops:
  0.6 3.5 %pack.6 = bf16[16,192,128]{2,1,0:T(8,128)(2,1)} custom-call(bf16[128,3072]{1,0:T(8,128)(2,1)} %refs_0_.6, bf16[128,3072]{1,0:T(8,128)(2,1)} %refs_1_.6), custom_call_target="tpu_custom_call" | custom-call | tf_op jit(solution)/shard_map/pack/pallas_call | solution.py:257
  4.1 9.2 %all-to-all-start = ((bf16[16,192,128]{2,1,0:T(8,128)(2,1)}), bf16[16,192,128]{2,1,0:T(8,128)(2,1)S(1)}, u32[]{:S(2)}, u32[]{:S(2)}) async-start(bf16[16,192,128]{2,1,0:T(8,128)(2,1)} %pack.6), calls=%async_computation | async-start | bytes 1572864 | tf_op jit(solution)/shard_map/all_to_all | solution.py:330
  13.3 3.5 %pack.4 = bf16[16,192,128]{2,1,0:T(8,128)(2,1)} custom-call(bf16[128,3072]{1,0:T(8,128)(2,1)} %refs_0_.6, bf16[128,3072]{1,0:T(8,128)(2,1)} %refs_1_.6), custom_call_target="tpu_custom_call" | custom-call | tf_op jit(solution)/shard_map/pack/pallas_call | solution.py:257
  16.7 3.5 %pack.7 = bf16[16,192,128]{2,1,0:T(8,128)(2,1)} custom-call(bf16[128,3072]{1,0:T(8,128)(2,1)} %refs_0_.7, bf16[128,3072]{1,0:T(8,128)(2,1)} %refs_1_.7), custom_call_target="tpu_custom_call" | custom-call | tf_op jit(solution)/shard_map/pack/pallas_call | solution.py:257
  20.2 3.5 %pack.5 = bf16[16,192,128]{2,1,0:T(8,128)(2,1)} custom-call(bf16[128,3072]{1,0:T(8,128)(2,1)} %refs_0_.7, bf16[128,3072]{1,0:T(8,128)(2,1)} %refs_1_.7), custom_call_target="tpu_custom_call" | custom-call | tf_op jit(solution)/shard_map/pack/pallas_call | solution.py:257
  23.7 12.2 %all-to-all-done.own = bf16[16,192,128]{2,1,0:T(8,128)(2,1)S(1)} async-done(((bf16[16,192,128]{2,1,0:T(8,128)(2,1)}), bf16[16,192,128]{2,1,0:T(8,128)(2,1)S(1)}, u32[]{:S(2)}, u32[]{:S(2)}) %all-to-all-start) | async-done | bytes 786464 | tf_op jit(solution)/shard_map/all_to_all | solution.py:330
  35.9 3.5 %all-to-all-start.1 = ((bf16[16,192,128]{2,1,0:T(8,128)(2,1)}), bf16[16,192,128]{2,1,0:T(8,128)(2,1)S(1)}, u32[]{:S(2)}, u32[]{:S(2)}) async-start(bf16[16,192,128]{2,1,0:T(8,128)(2,1)} %pack.5), calls=%async_computation.1 | async-start | bytes 1572864 | tf_op jit(solution)/shard_map/all_to_all | solution.py:330
  39.4 3.1 %collective-permute-start = (bf16[16,192,128]{2,1,0:T(8,128)(2,1)S(1)}, bf16[16,192,128]{2,1,0:T(8,128)(2,1)S(1)}, u32[]{:S(2)}, u32[]{:S(2)}) collective-permute-start(bf16[16,192,128]{2,1,0:T(8,128)(2,1)S(1)} %all-to-all-done.own), channel_id=1, source_target_pairs={{0,16},{1,17},{2,18},{3,19},{4,20},{5,21},{6,22},{7,23},{8,24},{9,... | collective-permute-start | bytes 2359304 | tf_op jit(solution)/shard_map/ppermute | solution.py:335
  42.6 20.2 %collective-permute-done.halo = bf16[16,192,128]{2,1,0:T(8,128)(2,1)S(1)} collective-permute-done((bf16[16,192,128]{2,1,0:T(8,128)(2,1)S(1)}, bf16[16,192,128]{2,1,0:T(8,128)(2,1)S(1)}, u32[]{:S(2)}, u32[]{:S(2)}) %collective-permute-start) | collective-permute-done | bytes 786464 | tf_op jit(solution)/shard_map/ppermute | solution.py:335
  62.8 7.1 %all-to-all-start.2 = ((bf16[16,192,128]{2,1,0:T(8,128)(2,1)}), bf16[16,192,128]{2,1,0:T(8,128)(2,1)S(1)}, u32[]{:S(2)}, u32[]{:S(2)}) async-start(bf16[16,192,128]{2,1,0:T(8,128)(2,1)} %pack.4), calls=%async_computation.2 | async-start | bytes 1572864 | tf_op jit(solution)/shard_map/all_to_all | solution.py:330
  69.9 13.2 %attend.2 = (bf16[16,96,128]{2,1,0:T(8,128)(2,1)}, bf16[16,192,128]{2,1,0:T(8,128)(2,1)S(1)}, f32[16,192,128]{2,1,0:T(8,128)}) custom-call(s32[32]{0:T(128)S(1)} %copy-done, s32[1]{0:T(128)} %bitcast.base, bf16[16,192,128]{2,1,0:T(8,128)(2,1)S(1)} %collective-permute-done.halo, bf16[16,192,128]{2,1,0:T(8,128)(2,1)S(1)} %all-to-all-done.own, ...), custom_call_target="tpu_custom_call" | custom-call | tf_op jit(solution)/shard_map/attend/pallas_call | solution.py:215
  84.0 8.6 %all-to-all-done.2.own = bf16[16,192,128]{2,1,0:T(8,128)(2,1)S(1)} async-done(((bf16[16,192,128]{2,1,0:T(8,128)(2,1)}), bf16[16,192,128]{2,1,0:T(8,128)(2,1)S(1)}, u32[]{:S(2)}, u32[]{:S(2)}) %all-to-all-start.2) | async-done | bytes 786464 | tf_op jit(solution)/shard_map/all_to_all | solution.py:330
  92.6 3.6 %all-to-all-start.3 = ((bf16[16,192,128]{2,1,0:T(8,128)(2,1)}), bf16[16,192,128]{2,1,0:T(8,128)(2,1)S(1)}, u32[]{:S(2)}, u32[]{:S(2)}) async-start(bf16[16,192,128]{2,1,0:T(8,128)(2,1)} %pack.7), calls=%async_computation.3 | async-start | bytes 1572864 | tf_op jit(solution)/shard_map/all_to_all | solution.py:330
  96.2 2.2 %collective-permute-start.2 = (bf16[16,192,128]{2,1,0:T(8,128)(2,1)S(1)}, bf16[16,192,128]{2,1,0:T(8,128)(2,1)S(1)}, u32[]{:S(2)}, u32[]{:S(2)}) collective-permute-start(bf16[16,192,128]{2,1,0:T(8,128)(2,1)S(1)} %copy-done.2), channel_id=1, source_target_pairs={{16,0},{17,1},{18,2},{19,3},{20,4},{21,5},{22,6},{23,7},{24,8},{25... | collective-permute-start | bytes 2359304 | tf_op jit(solution)/shard_map/ppermute | solution.py:335
  98.4 3.1 %collective-permute-start.1 = (bf16[16,192,128]{2,1,0:T(8,128)(2,1)S(1)}, bf16[16,192,128]{2,1,0:T(8,128)(2,1)S(1)}, u32[]{:S(2)}, u32[]{:S(2)}) collective-permute-start(bf16[16,192,128]{2,1,0:T(8,128)(2,1)S(1)} %all-to-all-done.2.own), channel_id=1, source_target_pairs={{0,16},{1,17},{2,18},{3,19},{4,20},{5,21},{6,22},{7,23},{8,24},{9,... | collective-permute-start | bytes 2359304 | tf_op jit(solution)/shard_map/ppermute | solution.py:335
  101.5 15.9 %collective-permute-done.2.refs_2_ = bf16[16,192,128]{2,1,0:T(8,128)(2,1)S(1)} collective-permute-done((bf16[16,192,128]{2,1,0:T(8,128)(2,1)S(1)}, bf16[16,192,128]{2,1,0:T(8,128)(2,1)S(1)}, u32[]{:S(2)}, u32[]{:S(2)}) %collective-permute-start.2) | collective-permute-done | bytes 786464 | tf_op jit(solution)/shard_map/ppermute | solution.py:335
  117.5 0.9 copy-done.4
  118.4 2.6 %total.2 = bf16[16,288,128]{2,1,0:T(8,128)(2,1)} custom-call(bf16[16,96,128]{2,1,0:T(8,128)(2,1)} %get-tuple-element.22.refs_0_, f32[16,192,128]{2,1,0:T(8,128)} %get-tuple-element.25.refs_1_, bf16[16,192,128]{2,1,0:T(8,128)(2,1)} %copy-done.4), custom_call_target="tpu_custom_call" | custom-call | tf_op jit(solution)/shard_map/total/pallas_call | solution.py:310
  121.6 7.3 %all-to-all-start.4 = ((bf16[16,288,128]{2,1,0:T(8,128)(2,1)}), bf16[16,288,128]{2,1,0:T(8,128)(2,1)S(1)}, u32[]{:S(2)}, u32[]{:S(2)}) async-start(bf16[16,288,128]{2,1,0:T(8,128)(2,1)} %total.2), calls=%async_computation.4 | async-start | bytes 2359296 | tf_op jit(solution)/shard_map/all_to_all | solution.py:330
  128.9 13.5 %attend.3 = (bf16[16,96,128]{2,1,0:T(8,128)(2,1)}, bf16[16,192,128]{2,1,0:T(8,128)(2,1)}, f32[16,192,128]{2,1,0:T(8,128)}) custom-call(s32[32]{0:T(128)S(1)} %copy-done, s32[1]{0:T(128)} %bitcast.base, bf16[16,192,128]{2,1,0:T(8,128)(2,1)S(1)} %collective-permute-done.1.halo, bf16[16,192,128]{2,1,0:T(8,128)(2,1)S(1)} %all-to-all-done.2.own, ...), custom_call_target="tpu_custom_call" | custom-call | tf_op jit(solution)/shard_map/attend/pallas_call | solution.py:215
  142.4 6.4 %collective-permute-start.3 = (bf16[16,192,128]{2,1,0:T(8,128)(2,1)}, bf16[16,192,128]{2,1,0:T(8,128)(2,1)S(1)}, u32[]{:S(2)}, u32[]{:S(2)}) collective-permute-start(bf16[16,192,128]{2,1,0:T(8,128)(2,1)} %get-tuple-element.31), channel_id=1, source_target_pairs={{16,0},{17,1},{18,2},{19,3},{20,4},{21,5},{22,6},{23,7},{24,8},{25... | collective-permute-start | bytes 2359304 | tf_op jit(solution)/shard_map/ppermute | solution.py:335
  148.8 10.7 %all-to-all-done.4.refs_0_ = bf16[16,288,128]{2,1,0:T(8,128)(2,1)S(1)} async-done(((bf16[16,288,128]{2,1,0:T(8,128)(2,1)}), bf16[16,288,128]{2,1,0:T(8,128)(2,1)S(1)}, u32[]{:S(2)}, u32[]{:S(2)}) %all-to-all-start.4) | async-done | bytes 1179680 | tf_op jit(solution)/shard_map/all_to_all | solution.py:330
  159.5 3.7 %all-to-all-start.5 = ((bf16[16,96,128]{2,1,0:T(8,128)(2,1)}), bf16[16,96,128]{2,1,0:T(8,128)(2,1)S(1)}, u32[]{:S(2)}, u32[]{:S(2)}) async-start(bf16[16,96,128]{2,1,0:T(8,128)(2,1)} %get-tuple-element.28), calls=%async_computation.5 | async-start | bytes 786432 | tf_op jit(solution)/shard_map/all_to_all | solution.py:330
  163.2 3.1 %collective-permute-done.3.refs_1_ = bf16[16,192,128]{2,1,0:T(8,128)(2,1)S(1)} collective-permute-done((bf16[16,192,128]{2,1,0:T(8,128)(2,1)}, bf16[16,192,128]{2,1,0:T(8,128)(2,1)S(1)}, u32[]{:S(2)}, u32[]{:S(2)}) %collective-permute-start.3) | collective-permute-done | bytes 786464 | tf_op jit(solution)/shard_map/ppermute | solution.py:335
  166.3 0.9 copy-done.3
  167.1 2.4 %total.3 = bf16[16,192,128]{2,1,0:T(8,128)(2,1)} custom-call(f32[16,192,128]{2,1,0:T(8,128)} %get-tuple-element.30.refs_0_, bf16[16,192,128]{2,1,0:T(8,128)(2,1)} %copy-done.3), custom_call_target="tpu_custom_call" | custom-call | tf_op jit(solution)/shard_map/total/pallas_call | solution.py:310
  169.5 8.2 %all-to-all-done.5.refs_0_ = bf16[16,96,128]{2,1,0:T(8,128)(2,1)S(1)} async-done(((bf16[16,96,128]{2,1,0:T(8,128)(2,1)}), bf16[16,96,128]{2,1,0:T(8,128)(2,1)S(1)}, u32[]{:S(2)}, u32[]{:S(2)}) %all-to-all-start.5) | async-done | bytes 393248 | tf_op jit(solution)/shard_map/all_to_all | solution.py:330
  177.7 3.5 %all-to-all-start.6 = ((bf16[16,192,128]{2,1,0:T(8,128)(2,1)}), bf16[16,192,128]{2,1,0:T(8,128)(2,1)S(1)}, u32[]{:S(2)}, u32[]{:S(2)}) async-start(bf16[16,192,128]{2,1,0:T(8,128)(2,1)} %total.3), calls=%async_computation.6 | async-start | bytes 1572864 | tf_op jit(solution)/shard_map/all_to_all | solution.py:330
  181.2 1.2 unpack.3
  182.4 0.9 unpack.4
  183.3 19.9 %all-to-all-done.6.refs_0_ = bf16[16,192,128]{2,1,0:T(8,128)(2,1)S(1)} async-done(((bf16[16,192,128]{2,1,0:T(8,128)(2,1)}), bf16[16,192,128]{2,1,0:T(8,128)(2,1)S(1)}, u32[]{:S(2)}, u32[]{:S(2)}) %all-to-all-start.6) | async-done | bytes 786464 | tf_op jit(solution)/shard_map/all_to_all | solution.py:330
  203.2 1.0 unpack.5
  (11 shorter events, 1.5 us)
Async XLA Ops:
  4.1 31.8 %all-to-all-start = ((bf16[16,192,128]{2,1,0:T(8,128)(2,1)}), bf16[16,192,128]{2,1,0:T(8,128)(2,1)S(1)}, u32[]{:S(2)}, u32[]{:S(2)}) async-start(bf16[16,192,128]{2,1,0:T(8,128)(2,1)} %pack.6), calls=%async_computation | async-start | bytes 1572864 | tf_op jit(solution)/shard_map/all_to_all | solution.py:330
  23.7 46.2 %copy-start = (s32[32]{0:T(128)S(1)}, s32[32]{0:T(128)}, u32[]{:S(2)}) copy-start(s32[32]{0:T(128)} %lens.3) | copy-start | bytes 388
  35.9 26.9 %all-to-all-start.1 = ((bf16[16,192,128]{2,1,0:T(8,128)(2,1)}), bf16[16,192,128]{2,1,0:T(8,128)(2,1)S(1)}, u32[]{:S(2)}, u32[]{:S(2)}) async-start(bf16[16,192,128]{2,1,0:T(8,128)(2,1)} %pack.5), calls=%async_computation.1 | async-start | bytes 1572864 | tf_op jit(solution)/shard_map/all_to_all | solution.py:330
  39.4 23.3 %collective-permute-start = (bf16[16,192,128]{2,1,0:T(8,128)(2,1)S(1)}, bf16[16,192,128]{2,1,0:T(8,128)(2,1)S(1)}, u32[]{:S(2)}, u32[]{:S(2)}) collective-permute-start(bf16[16,192,128]{2,1,0:T(8,128)(2,1)S(1)} %all-to-all-done.own), channel_id=1, source_target_pairs={{0,16},{1,17},{2,18},{3,19},{4,20},{5,21},{6,22},{7,23},{8,24},{9,... | collective-permute-start | bytes 2359304 | tf_op jit(solution)/shard_map/ppermute | solution.py:335
  62.8 29.8 %all-to-all-start.2 = ((bf16[16,192,128]{2,1,0:T(8,128)(2,1)}), bf16[16,192,128]{2,1,0:T(8,128)(2,1)S(1)}, u32[]{:S(2)}, u32[]{:S(2)}) async-start(bf16[16,192,128]{2,1,0:T(8,128)(2,1)} %pack.4), calls=%async_computation.2 | async-start | bytes 1572864 | tf_op jit(solution)/shard_map/all_to_all | solution.py:330
  83.1 0.9 copy-start.1
  92.6 3.7 %copy-start.2 = (bf16[16,192,128]{2,1,0:T(8,128)(2,1)S(1)}, bf16[16,192,128]{2,1,0:T(8,128)(2,1)}, u32[]{:S(2)}) copy-start(bf16[16,192,128]{2,1,0:T(8,128)(2,1)} %copy-done.1) | copy-start | bytes 2359300
  92.6 29.0 %all-to-all-start.3 = ((bf16[16,192,128]{2,1,0:T(8,128)(2,1)}), bf16[16,192,128]{2,1,0:T(8,128)(2,1)S(1)}, u32[]{:S(2)}, u32[]{:S(2)}) async-start(bf16[16,192,128]{2,1,0:T(8,128)(2,1)} %pack.7), calls=%async_computation.3 | async-start | bytes 1572864 | tf_op jit(solution)/shard_map/all_to_all | solution.py:330
  96.2 21.2 %collective-permute-start.2 = (bf16[16,192,128]{2,1,0:T(8,128)(2,1)S(1)}, bf16[16,192,128]{2,1,0:T(8,128)(2,1)S(1)}, u32[]{:S(2)}, u32[]{:S(2)}) collective-permute-start(bf16[16,192,128]{2,1,0:T(8,128)(2,1)S(1)} %copy-done.2), channel_id=1, source_target_pairs={{16,0},{17,1},{18,2},{19,3},{20,4},{21,5},{22,6},{23,7},{24,8},{25... | collective-permute-start | bytes 2359304 | tf_op jit(solution)/shard_map/ppermute | solution.py:335
  98.4 23.1 %collective-permute-start.1 = (bf16[16,192,128]{2,1,0:T(8,128)(2,1)S(1)}, bf16[16,192,128]{2,1,0:T(8,128)(2,1)S(1)}, u32[]{:S(2)}, u32[]{:S(2)}) collective-permute-start(bf16[16,192,128]{2,1,0:T(8,128)(2,1)S(1)} %all-to-all-done.2.own), channel_id=1, source_target_pairs={{0,16},{1,17},{2,18},{3,19},{4,20},{5,21},{6,22},{7,23},{8,24},{9,... | collective-permute-start | bytes 2359304 | tf_op jit(solution)/shard_map/ppermute | solution.py:335
  117.5 0.9 copy-start.4
  121.6 37.9 %all-to-all-start.4 = ((bf16[16,288,128]{2,1,0:T(8,128)(2,1)}), bf16[16,288,128]{2,1,0:T(8,128)(2,1)S(1)}, u32[]{:S(2)}, u32[]{:S(2)}) async-start(bf16[16,288,128]{2,1,0:T(8,128)(2,1)} %total.2), calls=%async_computation.4 | async-start | bytes 2359296 | tf_op jit(solution)/shard_map/all_to_all | solution.py:330
  142.4 23.9 %collective-permute-start.3 = (bf16[16,192,128]{2,1,0:T(8,128)(2,1)}, bf16[16,192,128]{2,1,0:T(8,128)(2,1)S(1)}, u32[]{:S(2)}, u32[]{:S(2)}) collective-permute-start(bf16[16,192,128]{2,1,0:T(8,128)(2,1)} %get-tuple-element.31), channel_id=1, source_target_pairs={{16,0},{17,1},{18,2},{19,3},{20,4},{21,5},{22,6},{23,7},{24,8},{25... | collective-permute-start | bytes 2359304 | tf_op jit(solution)/shard_map/ppermute | solution.py:335
  159.5 18.3 %all-to-all-start.5 = ((bf16[16,96,128]{2,1,0:T(8,128)(2,1)}), bf16[16,96,128]{2,1,0:T(8,128)(2,1)S(1)}, u32[]{:S(2)}, u32[]{:S(2)}) async-start(bf16[16,96,128]{2,1,0:T(8,128)(2,1)} %get-tuple-element.28), calls=%async_computation.5 | async-start | bytes 786432 | tf_op jit(solution)/shard_map/all_to_all | solution.py:330
  166.3 0.9 copy-start.3
  177.7 25.5 %all-to-all-start.6 = ((bf16[16,192,128]{2,1,0:T(8,128)(2,1)}), bf16[16,192,128]{2,1,0:T(8,128)(2,1)S(1)}, u32[]{:S(2)}, u32[]{:S(2)}) async-start(bf16[16,192,128]{2,1,0:T(8,128)(2,1)} %total.3), calls=%async_computation.6 | async-start | bytes 1572864 | tf_op jit(solution)/shard_map/all_to_all | solution.py:330

commit v4 on v3

--- a/solution.py
+++ b/solution.py
@@ -9,7 +9,7 @@
 HD = 96
 CH = 128
 PACK_VMEM = 56 * 1024 * 1024
-TOTAL_VMEM = 56 * 1024 * 1024
+TOTAL_VMEM = 16 * 1024 * 1024
 SUB = 2
 ATTEND_VMEM = 40 * 1024 * 1024
 FACTOR = 1.0 / math.sqrt(HD)
@@ -253,13 +253,12 @@
 def pack(arrays, half, plan, rows):
     tokens, columns = arrays[0].shape
     peers = columns // (2 * HD)
-    steps = peers // 4
     return pl.pallas_call(
         functools.partial(pack_kernel, plan),
-        grid=(steps,),
+        grid=(1,),
         out_shape=tuple(jax.ShapeDtypeStruct((peers, r, tokens), jnp.bfloat16) for r in rows),
-        in_specs=[pl.BlockSpec((tokens, 4 * HD), lambda i: (0, half * steps + i))] * len(arrays),
-        out_specs=tuple(pl.BlockSpec((4, r, tokens), lambda i: (i, 0, 0)) for r in rows),
+        in_specs=[pl.BlockSpec((tokens, columns // 2), lambda i: (0, half))] * len(arrays),
+        out_specs=tuple(pl.BlockSpec((peers, r, tokens), lambda i: (0, 0, 0)) for r in rows),
         compiler_params=pltpu.CompilerParams(vmem_limit_bytes=PACK_VMEM),
         name="pack",
     )(*arrays)

time: 207 us -> 205 us (level)
  Pallas kernels: 48.6 us -> 51.9 us
  starting transfers between devices: 52.8 us -> 50.3 us
    pallas_call x2, Pallas kernels: 26.7 us -> 37.8 us  [attend(): pl.pallas_call(functools.partial(attend_kernel, spec), grid=(nc // cq,),...]
    all_to_all x7, waiting for transfers between devices: 59.6 us -> 54.1 us  [exchange(): lax.all_to_all(x, 'head', split_axis=0, concat_axis=0, tiled=True, axis_i...]
    pallas_call x4, Pallas kernels: 13.9 us -> 9.01 us  [pack(): pl.pallas_call(functools.partial(pack_kernel, plan), grid=(1,), out_shape...]
    ppermute x4, starting transfers between devices: 14.8 us -> 11 us  [shift(): return lax.ppermute(x, ('blk', 'head'), route)]
    ppermute x4, waiting for transfers between devices: 39.8 us -> 43.3 us  [shift(): return lax.ppermute(x, ('blk', 'head'), route)]
    pallas_call x2, Pallas kernels: 5.01 us -> 2.07 us  [total(): pl.pallas_call(functools.partial(total_kernel, extra), grid=(steps,), out...]
  transfers between devices with their start and end apart: 11 -> 11, of which waited for: 9 -> 9; matrix products, arithmetic and copies ran while one was open for 0% -> 0% of each run, Pallas kernels for 22% -> 24%
where the time goes in v4:
time: 205 us; the launch traced here: 204 us
  waiting for transfers between devices  97.4 us (48%)
  Pallas kernels  51.9 us (25%)
  starting transfers between devices  50.3 us (25%)
  local copies, waits for them, and re-layouts  3.71 us (2%)
    all_to_all x7, waiting for transfers between devices, exchange(): lax.all_to_all(x, 'head', split_axis=0, concat_axis=0, tiled=True, axis_i...  54.1 us
    ppermute x4, waiting for transfers between devices, shift(): return lax.ppermute(x, ('blk', 'head'), route)  43.3 us
    all_to_all x7, starting transfers between devices, exchange(): lax.all_to_all(x, 'head', split_axis=0, concat_axis=0, tiled=True, axis_i...  39.4 us
    pallas_call x2, Pallas kernels, attend(): pl.pallas_call(functools.partial(attend_kernel, spec), grid=(nc // cq,),...  37.8 us
    ppermute x4, starting transfers between devices, shift(): return lax.ppermute(x, ('blk', 'head'), route)  11 us
    pallas_call x4, Pallas kernels, pack(): pl.pallas_call(functools.partial(pack_kernel, plan), grid=(1,), out_shape...  9.01 us
  transfers between devices with their start and end apart: 11, of which 9 were waited for; matrix products, arithmetic and copies ran while one was open for 0% of the time, Pallas kernels for 24%

profile of v4, /device:TPU:17, one launch (start us, length us, event | category | flops | bytes accessed | tf_op | source)
XLA Modules:
  0.0 204.1 jit_solution(4041737354811691988)
XLA Ops:
  0.6 2.3 %pack.6 = bf16[16,192,128]{2,1,0:T(8,128)(2,1)} custom-call(bf16[128,3072]{1,0:T(8,128)(2,1)} %refs_0_.6, bf16[128,3072]{1,0:T(8,128)(2,1)} %refs_1_.6), custom_call_target="tpu_custom_call" | custom-call | tf_op jit(solution)/shard_map/pack/pallas_call | solution.py:256
  2.9 9.2 %all-to-all-start = ((bf16[16,192,128]{2,1,0:T(8,128)(2,1)}), bf16[16,192,128]{2,1,0:T(8,128)(2,1)S(1)}, u32[]{:S(2)}, u32[]{:S(2)}) async-start(bf16[16,192,128]{2,1,0:T(8,128)(2,1)} %pack.6), calls=%async_computation | async-start | bytes 1572864 | tf_op jit(solution)/shard_map/all_to_all | solution.py:329
  12.0 2.2 %pack.4 = bf16[16,192,128]{2,1,0:T(8,128)(2,1)} custom-call(bf16[128,3072]{1,0:T(8,128)(2,1)} %refs_0_.6, bf16[128,3072]{1,0:T(8,128)(2,1)} %refs_1_.6), custom_call_target="tpu_custom_call" | custom-call | tf_op jit(solution)/shard_map/pack/pallas_call | solution.py:256
  14.3 2.2 %pack.7 = bf16[16,192,128]{2,1,0:T(8,128)(2,1)} custom-call(bf16[128,3072]{1,0:T(8,128)(2,1)} %refs_0_.7, bf16[128,3072]{1,0:T(8,128)(2,1)} %refs_1_.7), custom_call_target="tpu_custom_call" | custom-call | tf_op jit(solution)/shard_map/pack/pallas_call | solution.py:256
  16.5 2.3 %pack.5 = bf16[16,192,128]{2,1,0:T(8,128)(2,1)} custom-call(bf16[128,3072]{1,0:T(8,128)(2,1)} %refs_0_.7, bf16[128,3072]{1,0:T(8,128)(2,1)} %refs_1_.7), custom_call_target="tpu_custom_call" | custom-call | tf_op jit(solution)/shard_map/pack/pallas_call | solution.py:256
  18.8 15.9 %all-to-all-done.own = bf16[16,192,128]{2,1,0:T(8,128)(2,1)S(1)} async-done(((bf16[16,192,128]{2,1,0:T(8,128)(2,1)}), bf16[16,192,128]{2,1,0:T(8,128)(2,1)S(1)}, u32[]{:S(2)}, u32[]{:S(2)}) %all-to-all-start) | async-done | bytes 786464 | tf_op jit(solution)/shard_map/all_to_all | solution.py:329
  34.7 3.5 %all-to-all-start.1 = ((bf16[16,192,128]{2,1,0:T(8,128)(2,1)}), bf16[16,192,128]{2,1,0:T(8,128)(2,1)S(1)}, u32[]{:S(2)}, u32[]{:S(2)}) async-start(bf16[16,192,128]{2,1,0:T(8,128)(2,1)} %pack.5), calls=%async_computation.1 | async-start | bytes 1572864 | tf_op jit(solution)/shard_map/all_to_all | solution.py:329
  38.2 3.1 %collective-permute-start = (bf16[16,192,128]{2,1,0:T(8,128)(2,1)S(1)}, bf16[16,192,128]{2,1,0:T(8,128)(2,1)S(1)}, u32[]{:S(2)}, u32[]{:S(2)}) collective-permute-start(bf16[16,192,128]{2,1,0:T(8,128)(2,1)S(1)} %all-to-all-done.own), channel_id=1, source_target_pairs={{0,16},{1,17},{2,18},{3,19},{4,20},{5,21},{6,22},{7,23},{8,24},{9,... | collective-permute-start | bytes 2359304 | tf_op jit(solution)/shard_map/ppermute | solution.py:334
  41.3 20.2 %collective-permute-done.halo = bf16[16,192,128]{2,1,0:T(8,128)(2,1)S(1)} collective-permute-done((bf16[16,192,128]{2,1,0:T(8,128)(2,1)S(1)}, bf16[16,192,128]{2,1,0:T(8,128)(2,1)S(1)}, u32[]{:S(2)}, u32[]{:S(2)}) %collective-permute-start) | collective-permute-done | bytes 786464 | tf_op jit(solution)/shard_map/ppermute | solution.py:334
  61.6 7.1 %all-to-all-start.2 = ((bf16[16,192,128]{2,1,0:T(8,128)(2,1)}), bf16[16,192,128]{2,1,0:T(8,128)(2,1)S(1)}, u32[]{:S(2)}, u32[]{:S(2)}) async-start(bf16[16,192,128]{2,1,0:T(8,128)(2,1)} %pack.4), calls=%async_computation.2 | async-start | bytes 1572864 | tf_op jit(solution)/shard_map/all_to_all | solution.py:329
  68.7 18.8 %attend.2 = (bf16[16,96,128]{2,1,0:T(8,128)(2,1)}, bf16[16,192,128]{2,1,0:T(8,128)(2,1)S(1)}, f32[16,192,128]{2,1,0:T(8,128)}) custom-call(s32[32]{0:T(128)S(1)} %copy-done.3, s32[1]{0:T(128)} %bitcast.base, bf16[16,192,128]{2,1,0:T(8,128)(2,1)S(1)} %collective-permute-done.halo, bf16[16,192,128]{2,1,0:T(8,128)(2,1)S(1)} %all-to-all-done.own, ...), custom_call_target="tpu_custom_call" | custom-call | tf_op jit(solution)/shard_map/attend/pallas_call | solution.py:215
  88.3 3.0 %all-to-all-done.2.own = bf16[16,192,128]{2,1,0:T(8,128)(2,1)S(1)} async-done(((bf16[16,192,128]{2,1,0:T(8,128)(2,1)}), bf16[16,192,128]{2,1,0:T(8,128)(2,1)S(1)}, u32[]{:S(2)}, u32[]{:S(2)}) %all-to-all-start.2) | async-done | bytes 786464 | tf_op jit(solution)/shard_map/all_to_all | solution.py:329
  91.4 4.3 %all-to-all-start.3 = ((bf16[16,192,128]{2,1,0:T(8,128)(2,1)}), bf16[16,192,128]{2,1,0:T(8,128)(2,1)S(1)}, u32[]{:S(2)}, u32[]{:S(2)}) async-start(bf16[16,192,128]{2,1,0:T(8,128)(2,1)} %pack.7), calls=%async_computation.3 | async-start | bytes 1572864 | tf_op jit(solution)/shard_map/all_to_all | solution.py:329
  95.7 2.2 %collective-permute-start.2 = (bf16[16,192,128]{2,1,0:T(8,128)(2,1)S(1)}, bf16[16,192,128]{2,1,0:T(8,128)(2,1)S(1)}, u32[]{:S(2)}, u32[]{:S(2)}) collective-permute-start(bf16[16,192,128]{2,1,0:T(8,128)(2,1)S(1)} %copy-done.5), channel_id=1, source_target_pairs={{16,0},{17,1},{18,2},{19,3},{20,4},{21,5},{22,6},{23,7},{24,8},{25... | collective-permute-start | bytes 2359304 | tf_op jit(solution)/shard_map/ppermute | solution.py:334
  97.9 3.1 %collective-permute-start.1 = (bf16[16,192,128]{2,1,0:T(8,128)(2,1)S(1)}, bf16[16,192,128]{2,1,0:T(8,128)(2,1)S(1)}, u32[]{:S(2)}, u32[]{:S(2)}) collective-permute-start(bf16[16,192,128]{2,1,0:T(8,128)(2,1)S(1)} %all-to-all-done.2.own), channel_id=1, source_target_pairs={{0,16},{1,17},{2,18},{3,19},{4,20},{5,21},{6,22},{7,23},{8,24},{9,... | collective-permute-start | bytes 2359304 | tf_op jit(solution)/shard_map/ppermute | solution.py:334
  101.0 15.7 %collective-permute-done.2.refs_2_ = bf16[16,192,128]{2,1,0:T(8,128)(2,1)S(1)} collective-permute-done((bf16[16,192,128]{2,1,0:T(8,128)(2,1)S(1)}, bf16[16,192,128]{2,1,0:T(8,128)(2,1)S(1)}, u32[]{:S(2)}, u32[]{:S(2)}) %collective-permute-start.2) | collective-permute-done | bytes 786464 | tf_op jit(solution)/shard_map/ppermute | solution.py:334
  116.7 1.4 copy-done.1
  118.1 1.1 total.2
  119.2 1.4 collective-permute-done.1.halo
  120.7 8.0 %all-to-all-start.4 = ((bf16[16,288,128]{2,1,0:T(8,128)(2,1)}), bf16[16,288,128]{2,1,0:T(8,128)(2,1)S(1)}, u32[]{:S(2)}, u32[]{:S(2)}) async-start(bf16[16,288,128]{2,1,0:T(8,128)(2,1)} %total.2), calls=%async_computation.4 | async-start | bytes 2359296 | tf_op jit(solution)/shard_map/all_to_all | solution.py:329
  128.7 19.0 %attend.3 = (bf16[16,96,128]{2,1,0:T(8,128)(2,1)}, bf16[16,192,128]{2,1,0:T(8,128)(2,1)}, f32[16,192,128]{2,1,0:T(8,128)}) custom-call(s32[32]{0:T(128)S(1)} %copy-done.3, s32[1]{0:T(128)} %bitcast.base, bf16[16,192,128]{2,1,0:T(8,128)(2,1)S(1)} %collective-permute-done.1.halo, bf16[16,192,128]{2,1,0:T(8,128)(2,1)S(1)} %all-to-all-done.2.own, ...), custom_call_target="tpu_custom_call" | custom-call | tf_op jit(solution)/shard_map/attend/pallas_call | solution.py:215
  147.7 2.5 %collective-permute-start.3 = (bf16[16,192,128]{2,1,0:T(8,128)(2,1)}, bf16[16,192,128]{2,1,0:T(8,128)(2,1)S(1)}, u32[]{:S(2)}, u32[]{:S(2)}) collective-permute-start(bf16[16,192,128]{2,1,0:T(8,128)(2,1)} %get-tuple-element.31), channel_id=1, source_target_pairs={{16,0},{17,1},{18,2},{19,3},{20,4},{21,5},{22,6},{23,7},{24,8},{25... | collective-permute-start | bytes 2359304 | tf_op jit(solution)/shard_map/ppermute | solution.py:334
  150.3 9.0 %all-to-all-done.4.refs_0_ = bf16[16,288,128]{2,1,0:T(8,128)(2,1)S(1)} async-done(((bf16[16,288,128]{2,1,0:T(8,128)(2,1)}), bf16[16,288,128]{2,1,0:T(8,128)(2,1)S(1)}, u32[]{:S(2)}, u32[]{:S(2)}) %all-to-all-start.4) | async-done | bytes 1179680 | tf_op jit(solution)/shard_map/all_to_all | solution.py:329
  159.3 3.7 %all-to-all-start.5 = ((bf16[16,96,128]{2,1,0:T(8,128)(2,1)}), bf16[16,96,128]{2,1,0:T(8,128)(2,1)S(1)}, u32[]{:S(2)}, u32[]{:S(2)}) async-start(bf16[16,96,128]{2,1,0:T(8,128)(2,1)} %get-tuple-element.28), calls=%async_computation.5 | async-start | bytes 786432 | tf_op jit(solution)/shard_map/all_to_all | solution.py:329
  163.0 6.0 %collective-permute-done.3.refs_1_ = bf16[16,192,128]{2,1,0:T(8,128)(2,1)S(1)} collective-permute-done((bf16[16,192,128]{2,1,0:T(8,128)(2,1)}, bf16[16,192,128]{2,1,0:T(8,128)(2,1)S(1)}, u32[]{:S(2)}, u32[]{:S(2)}) %collective-permute-start.3) | collective-permute-done | bytes 786464 | tf_op jit(solution)/shard_map/ppermute | solution.py:334
  168.9 1.4 copy-done
  170.3 1.0 total.3
  171.3 6.2 %all-to-all-done.5.refs_0_ = bf16[16,96,128]{2,1,0:T(8,128)(2,1)S(1)} async-done(((bf16[16,96,128]{2,1,0:T(8,128)(2,1)}), bf16[16,96,128]{2,1,0:T(8,128)(2,1)S(1)}, u32[]{:S(2)}, u32[]{:S(2)}) %all-to-all-start.5) | async-done | bytes 393248 | tf_op jit(solution)/shard_map/all_to_all | solution.py:329
  177.5 3.5 %all-to-all-start.6 = ((bf16[16,192,128]{2,1,0:T(8,128)(2,1)}), bf16[16,192,128]{2,1,0:T(8,128)(2,1)S(1)}, u32[]{:S(2)}, u32[]{:S(2)}) async-start(bf16[16,192,128]{2,1,0:T(8,128)(2,1)} %total.3), calls=%async_computation.6 | async-start | bytes 1572864 | tf_op jit(solution)/shard_map/all_to_all | solution.py:329
  181.0 1.2 unpack.3
  183.1 19.9 %all-to-all-done.6.refs_0_ = bf16[16,192,128]{2,1,0:T(8,128)(2,1)S(1)} async-done(((bf16[16,192,128]{2,1,0:T(8,128)(2,1)}), bf16[16,192,128]{2,1,0:T(8,128)(2,1)S(1)}, u32[]{:S(2)}, u32[]{:S(2)}) %all-to-all-start.6) | async-done | bytes 786464 | tf_op jit(solution)/shard_map/all_to_all | solution.py:329
  203.0 1.0 unpack.5
  (13 shorter events, 1.8 us)
Async XLA Ops:
  2.9 31.8 %all-to-all-start = ((bf16[16,192,128]{2,1,0:T(8,128)(2,1)}), bf16[16,192,128]{2,1,0:T(8,128)(2,1)S(1)}, u32[]{:S(2)}, u32[]{:S(2)}) async-start(bf16[16,192,128]{2,1,0:T(8,128)(2,1)} %pack.6), calls=%async_computation | async-start | bytes 1572864 | tf_op jit(solution)/shard_map/all_to_all | solution.py:329
  18.8 49.9 %copy-start.3 = (s32[32]{0:T(128)S(1)}, s32[32]{0:T(128)}, u32[]{:S(2)}) copy-start(s32[32]{0:T(128)} %lens.3) | copy-start | bytes 388
  34.7 26.9 %all-to-all-start.1 = ((bf16[16,192,128]{2,1,0:T(8,128)(2,1)}), bf16[16,192,128]{2,1,0:T(8,128)(2,1)S(1)}, u32[]{:S(2)}, u32[]{:S(2)}) async-start(bf16[16,192,128]{2,1,0:T(8,128)(2,1)} %pack.5), calls=%async_computation.1 | async-start | bytes 1572864 | tf_op jit(solution)/shard_map/all_to_all | solution.py:329
  38.2 23.3 %collective-permute-start = (bf16[16,192,128]{2,1,0:T(8,128)(2,1)S(1)}, bf16[16,192,128]{2,1,0:T(8,128)(2,1)S(1)}, u32[]{:S(2)}, u32[]{:S(2)}) collective-permute-start(bf16[16,192,128]{2,1,0:T(8,128)(2,1)S(1)} %all-to-all-done.own), channel_id=1, source_target_pairs={{0,16},{1,17},{2,18},{3,19},{4,20},{5,21},{6,22},{7,23},{8,24},{9,... | collective-permute-start | bytes 2359304 | tf_op jit(solution)/shard_map/ppermute | solution.py:334
  61.6 29.8 %all-to-all-start.2 = ((bf16[16,192,128]{2,1,0:T(8,128)(2,1)}), bf16[16,192,128]{2,1,0:T(8,128)(2,1)S(1)}, u32[]{:S(2)}, u32[]{:S(2)}) async-start(bf16[16,192,128]{2,1,0:T(8,128)(2,1)} %pack.4), calls=%async_computation.2 | async-start | bytes 1572864 | tf_op jit(solution)/shard_map/all_to_all | solution.py:329
  87.5 0.9 copy-start.4
  88.3 28.4 %copy-start.2 = (bf16[16,96,128]{2,1,0:T(8,128)(2,1)S(1)}, bf16[16,96,128]{2,1,0:T(8,128)(2,1)}, u32[]{:S(2)}) copy-start(bf16[16,96,128]{2,1,0:T(8,128)(2,1)} %get-tuple-element.22.refs_0_) | copy-start | bytes 1179652
  91.4 4.3 %copy-start.5 = (bf16[16,192,128]{2,1,0:T(8,128)(2,1)S(1)}, bf16[16,192,128]{2,1,0:T(8,128)(2,1)}, u32[]{:S(2)}) copy-start(bf16[16,192,128]{2,1,0:T(8,128)(2,1)} %copy-done.4) | copy-start | bytes 2359300
  91.4 29.3 %all-to-all-start.3 = ((bf16[16,192,128]{2,1,0:T(8,128)(2,1)}), bf16[16,192,128]{2,1,0:T(8,128)(2,1)S(1)}, u32[]{:S(2)}, u32[]{:S(2)}) async-start(bf16[16,192,128]{2,1,0:T(8,128)(2,1)} %pack.7), calls=%async_computation.3 | async-start | bytes 1572864 | tf_op jit(solution)/shard_map/all_to_all | solution.py:329
  95.7 21.0 %collective-permute-start.2 = (bf16[16,192,128]{2,1,0:T(8,128)(2,1)S(1)}, bf16[16,192,128]{2,1,0:T(8,128)(2,1)S(1)}, u32[]{:S(2)}, u32[]{:S(2)}) collective-permute-start(bf16[16,192,128]{2,1,0:T(8,128)(2,1)S(1)} %copy-done.5), channel_id=1, source_target_pairs={{16,0},{17,1},{18,2},{19,3},{20,4},{21,5},{22,6},{23,7},{24,8},{25... | collective-permute-start | bytes 2359304 | tf_op jit(solution)/shard_map/ppermute | solution.py:334
  97.9 22.8 %collective-permute-start.1 = (bf16[16,192,128]{2,1,0:T(8,128)(2,1)S(1)}, bf16[16,192,128]{2,1,0:T(8,128)(2,1)S(1)}, u32[]{:S(2)}, u32[]{:S(2)}) collective-permute-start(bf16[16,192,128]{2,1,0:T(8,128)(2,1)S(1)} %all-to-all-done.2.own), channel_id=1, source_target_pairs={{0,16},{1,17},{2,18},{3,19},{4,20},{5,21},{6,22},{7,23},{8,24},{9,... | collective-permute-start | bytes 2359304 | tf_op jit(solution)/shard_map/ppermute | solution.py:334
  116.7 1.4 copy-start.1
  120.7 38.6 %all-to-all-start.4 = ((bf16[16,288,128]{2,1,0:T(8,128)(2,1)}), bf16[16,288,128]{2,1,0:T(8,128)(2,1)S(1)}, u32[]{:S(2)}, u32[]{:S(2)}) async-start(bf16[16,288,128]{2,1,0:T(8,128)(2,1)} %total.2), calls=%async_computation.4 | async-start | bytes 2359296 | tf_op jit(solution)/shard_map/all_to_all | solution.py:329
  147.7 21.2 %collective-permute-start.3 = (bf16[16,192,128]{2,1,0:T(8,128)(2,1)}, bf16[16,192,128]{2,1,0:T(8,128)(2,1)S(1)}, u32[]{:S(2)}, u32[]{:S(2)}) collective-permute-start(bf16[16,192,128]{2,1,0:T(8,128)(2,1)} %get-tuple-element.31), channel_id=1, source_target_pairs={{16,0},{17,1},{18,2},{19,3},{20,4},{21,5},{22,6},{23,7},{24,8},{25... | collective-permute-start | bytes 2359304 | tf_op jit(solution)/shard_map/ppermute | solution.py:334
  159.3 18.3 %all-to-all-start.5 = ((bf16[16,96,128]{2,1,0:T(8,128)(2,1)}), bf16[16,96,128]{2,1,0:T(8,128)(2,1)S(1)}, u32[]{:S(2)}, u32[]{:S(2)}) async-start(bf16[16,96,128]{2,1,0:T(8,128)(2,1)} %get-tuple-element.28), calls=%async_computation.5 | async-start | bytes 786432 | tf_op jit(solution)/shard_map/all_to_all | solution.py:329
  168.9 1.4 copy-start
  177.5 25.5 %all-to-all-start.6 = ((bf16[16,192,128]{2,1,0:T(8,128)(2,1)}), bf16[16,192,128]{2,1,0:T(8,128)(2,1)S(1)}, u32[]{:S(2)}, u32[]{:S(2)}) async-start(bf16[16,192,128]{2,1,0:T(8,128)(2,1)} %total.3), calls=%async_computation.6 | async-start | bytes 1572864 | tf_op jit(solution)/shard_map/all_to_all | solution.py:329

commit v5 on v4

--- a/solution.py
+++ b/solution.py
@@ -250,14 +250,14 @@
                 outs[which][4 * m + n, row : row + HD, :] = block[n * HD : (n + 1) * HD]
 
 
-def pack(arrays, half, plan, rows):
+def pack(arrays, halves, plan, rows):
     tokens, columns = arrays[0].shape
     peers = columns // (2 * HD)
     return pl.pallas_call(
         functools.partial(pack_kernel, plan),
         grid=(1,),
         out_shape=tuple(jax.ShapeDtypeStruct((peers, r, tokens), jnp.bfloat16) for r in rows),
-        in_specs=[pl.BlockSpec((tokens, columns // 2), lambda i: (0, half))] * len(arrays),
+        in_specs=[pl.BlockSpec((tokens, columns // 2), lambda i, h=h: (0, h)) for h in halves],
         out_specs=tuple(pl.BlockSpec((peers, r, tokens), lambda i: (0, 0, 0)) for r in rows),
         compiler_params=pltpu.CompilerParams(vmem_limit_bytes=PACK_VMEM),
         name="pack",
@@ -341,30 +341,30 @@
     pair = ((0, 0), (0, HD))
 
     def pack_pair(first, second, half):
-        return pack((first, second), half, pair, (2 * HD,))[0]
+        return pack((first, second), (half, half), pair, (2 * HD,))[0]
 
     send_kv_a = pack_pair(keys_in, values, 0)
-    send_q_a = pack_pair(queries, out_grad, 0)
-    send_kv_b = pack_pair(keys_in, values, 1)
     send_q_b = pack_pair(queries, out_grad, 1)
+    four = ((0, 0), (0, HD), (0, 2 * HD), (0, 3 * HD))
+    (send_mid,) = pack((queries, out_grad, keys_in, values), (0, 0, 1, 1), four, (4 * HD,))
 
     own_a = exchange(send_kv_a)
     halo_a = shift(own_a, up)
-    rows_a = exchange(after(send_q_a, own_a, send_kv_b, send_q_b))
-    own_b = exchange(after(send_kv_b, rows_a, halo_a))
+    middle = exchange(after(send_mid, own_a, send_q_b))
+    own_b = middle[:, 2 * HD :, :]
     halo_b = shift(own_b, up)
-    dq_a, back_a, mine_a = attend(doc_lengths, base, halo_a, own_a, rows_a, 0)
+    rows_b = exchange(after(send_q_b, middle, halo_a))
+    dq_a, back_a, mine_a = attend(doc_lengths, base, halo_a, own_a, middle, 0)
     got_a = shift(back_a, down)
-    rows_b = exchange(after(send_q_b, own_b, dq_a))
-    sum_a = total((dq_a,), mine_a, got_a)
-    out_a = exchange(after(sum_a, rows_b, halo_b))
+    out_q = exchange(after(dq_a, rows_b, halo_b))
     dq_b, back_b, mine_b = attend(doc_lengths, base, halo_b, own_b, rows_b, 0)
     got_b = shift(back_b, down)
-    out_q = exchange(after(dq_b, out_a))
+    sum_a = total((dq_b,), mine_a, got_a)
+    out_a = exchange(after(sum_a, out_q))
     sum_b = total((), mine_b, got_b)
-    out_b = exchange(after(sum_b, out_q))
-    grad_q, grad_k, grad_v = unpack((out_a,), 0, ((0, 0), (0, HD), (0, 2 * HD)))
-    (grad_q,) = unpack((out_q,), 1, ((0, 0),), (grad_q,))
+    out_b = exchange(after(sum_b, out_a))
+    grad_q, grad_k, grad_v = unpack((out_q, out_a), 0, ((0, 0), (1, HD), (1, 2 * HD)))
+    (grad_q,) = unpack((out_a,), 1, ((0, 0),), (grad_q,))
     grad_k, grad_v = unpack((out_b,), 1, pair, (grad_k, grad_v))
     return grad_q, grad_k, grad_v
 

time: 205 us -> 204 us (level)
  Pallas kernels: 51.9 us -> 49.1 us
    all_to_all x7 -> x6, waiting for transfers between devices: 54.1 us -> 60.1 us  [exchange(): lax.all_to_all(x, 'head', split_axis=0, concat_axis=0, tiled=True, axis_i...]
    ppermute x4, waiting for transfers between devices: 43.3 us -> 39.3 us  [shift(): return lax.ppermute(x, ('blk', 'head'), route)]
    all_to_all x7 -> x6, starting transfers between devices: 39.4 us -> 36 us  [exchange(): lax.all_to_all(x, 'head', split_axis=0, concat_axis=0, tiled=True, axis_i...]
    ppermute x4, starting transfers between devices: 11 us -> 13.2 us  [shift(): return lax.ppermute(x, ('blk', 'head'), route)]
    pallas_call x4 -> x3, Pallas kernels: 9.01 us -> 7.49 us  [pack(): pl.pallas_call(functools.partial(pack_kernel, plan), grid=(1,), out_shape...]
  transfers between devices with their start and end apart: 11 -> 10, of which waited for: 9 -> 6; matrix products, arithmetic and copies ran while one was open for 0% -> 0% of each run, Pallas kernels for 24% -> 23%
where the time goes in v5:
time: 204 us; the launch traced here: 203 us
  waiting for transfers between devices  99.4 us (49%)
  starting transfers between devices  49.2 us (24%)
  Pallas kernels  49.1 us (24%)
  local copies, waits for them, and re-layouts  4.84 us (2%)
    all_to_all x6, waiting for transfers between devices, exchange(): lax.all_to_all(x, 'head', split_axis=0, concat_axis=0, tiled=True, axis_i...  60.1 us
    ppermute x4, waiting for transfers between devices, shift(): return lax.ppermute(x, ('blk', 'head'), route)  39.3 us
    pallas_call x2, Pallas kernels, attend(): pl.pallas_call(functools.partial(attend_kernel, spec), grid=(nc // cq,),...  36.5 us
    all_to_all x6, starting transfers between devices, exchange(): lax.all_to_all(x, 'head', split_axis=0, concat_axis=0, tiled=True, axis_i...  36 us
    ppermute x4, starting transfers between devices, shift(): return lax.ppermute(x, ('blk', 'head'), route)  13.2 us
    pallas_call x3, Pallas kernels, pack(): pl.pallas_call(functools.partial(pack_kernel, plan), grid=(1,), out_shape...  7.49 us
  transfers between devices with their start and end apart: 10, of which 6 were waited for; matrix products, arithmetic and copies ran while one was open for 0% of the time, Pallas kernels for 23%

profile of v5, /device:TPU:17, one launch (start us, length us, event | category | flops | bytes accessed | tf_op | source)
XLA Modules:
  0.0 203.4 jit_solution(6086201064220382728)
XLA Ops:
  0.6 2.3 %pack.4 = bf16[16,192,128]{2,1,0:T(8,128)(2,1)} custom-call(bf16[128,3072]{1,0:T(8,128)(2,1)} %refs_0_.4, bf16[128,3072]{1,0:T(8,128)(2,1)} %refs_1_.4), custom_call_target="tpu_custom_call" | custom-call | tf_op jit(solution)/shard_map/pack/pallas_call | solution.py:256
  2.9 9.2 %all-to-all-start = ((bf16[16,192,128]{2,1,0:T(8,128)(2,1)}), bf16[16,192,128]{2,1,0:T(8,128)(2,1)S(1)}, u32[]{:S(2)}, u32[]{:S(2)}) async-start(bf16[16,192,128]{2,1,0:T(8,128)(2,1)} %pack.4), calls=%async_computation | async-start | bytes 1572864 | tf_op jit(solution)/shard_map/all_to_all | solution.py:329
  12.0 2.2 %pack.5 = bf16[16,192,128]{2,1,0:T(8,128)(2,1)} custom-call(bf16[128,3072]{1,0:T(8,128)(2,1)} %refs_0_.5, bf16[128,3072]{1,0:T(8,128)(2,1)} %refs_1_.5), custom_call_target="tpu_custom_call" | custom-call | tf_op jit(solution)/shard_map/pack/pallas_call | solution.py:256
  14.3 3.0 %pack.3 = bf16[16,384,128]{2,1,0:T(8,128)(2,1)} custom-call(bf16[128,3072]{1,0:T(8,128)(2,1)} %refs_0_.5, bf16[128,3072]{1,0:T(8,128)(2,1)} %refs_1_.5, bf16[128,3072]{1,0:T(8,128)(2,1)} %refs_0_.4, bf16[128,3072]{1,0:T(8,128)(2,1)} %refs_1_.4), custom_call_target="tpu_custom_call" | custom-call | tf_op jit(solution)/shard_map/pack/pallas_call | solution.py:256
  17.3 17.4 %all-to-all-done.own = bf16[16,192,128]{2,1,0:T(8,128)(2,1)S(1)} async-done(((bf16[16,192,128]{2,1,0:T(8,128)(2,1)}), bf16[16,192,128]{2,1,0:T(8,128)(2,1)S(1)}, u32[]{:S(2)}, u32[]{:S(2)}) %all-to-all-start) | async-done | bytes 786464 | tf_op jit(solution)/shard_map/all_to_all | solution.py:329
  34.7 3.6 %all-to-all-start.1 = ((bf16[16,384,128]{2,1,0:T(8,128)(2,1)}), bf16[16,384,128]{2,1,0:T(8,128)(2,1)S(1)}, u32[]{:S(2)}, u32[]{:S(2)}) async-start(bf16[16,384,128]{2,1,0:T(8,128)(2,1)} %pack.3), calls=%async_computation.1 | async-start | bytes 3145728 | tf_op jit(solution)/shard_map/all_to_all | solution.py:329
  38.3 0.0 copy-start.5
  38.3 3.1 %collective-permute-start.1 = (bf16[16,192,128]{2,1,0:T(8,128)(2,1)S(1)}, bf16[16,192,128]{2,1,0:T(8,128)(2,1)S(1)}, u32[]{:S(2)}, u32[]{:S(2)}) collective-permute-start(bf16[16,192,128]{2,1,0:T(8,128)(2,1)S(1)} %all-to-all-done.own), channel_id=1, source_target_pairs={{0,16},{1,17},{2,18},{3,19},{4,20},{5,21},{6,22},{7,23},{8,24},{9,... | collective-permute-start | bytes 2359304 | tf_op jit(solution)/shard_map/ppermute | solution.py:334
  41.5 20.3 %collective-permute-done.1.halo = bf16[16,192,128]{2,1,0:T(8,128)(2,1)S(1)} collective-permute-done((bf16[16,192,128]{2,1,0:T(8,128)(2,1)S(1)}, bf16[16,192,128]{2,1,0:T(8,128)(2,1)S(1)}, u32[]{:S(2)}, u32[]{:S(2)}) %collective-permute-start.1) | collective-permute-done | bytes 786464 | tf_op jit(solution)/shard_map/ppermute | solution.py:334
  61.8 0.9 copy-done.2
  62.6 13.7 %all-to-all-done.1.qd = bf16[16,384,128]{2,1,0:T(8,128)(2,1)S(1)} async-done(((bf16[16,384,128]{2,1,0:T(8,128)(2,1)}), bf16[16,384,128]{2,1,0:T(8,128)(2,1)S(1)}, u32[]{:S(2)}, u32[]{:S(2)}) %all-to-all-start.1) | async-done | bytes 1572896 | tf_op jit(solution)/shard_map/all_to_all | solution.py:329
  76.3 4.3 %all-to-all-start.2 = ((bf16[16,192,128]{2,1,0:T(8,128)(2,1)}), bf16[16,192,128]{2,1,0:T(8,128)(2,1)S(1)}, u32[]{:S(2)}, u32[]{:S(2)}) async-start(bf16[16,192,128]{2,1,0:T(8,128)(2,1)} %pack.5), calls=%async_computation.2 | async-start | bytes 1572864 | tf_op jit(solution)/shard_map/all_to_all | solution.py:329
  80.6 0.9 slice.4.own
  81.5 3.1 %collective-permute-start = (bf16[16,192,128]{2,1,0:T(8,128)(2,1)}, bf16[16,192,128]{2,1,0:T(8,128)(2,1)}, u32[]{:S(2)}, u32[]{:S(2)}) collective-permute-start(bf16[16,192,128]{2,1,0:T(8,128)(2,1)} %slice.4.own), channel_id=1, source_target_pairs={{0,16},{1,17},{2,18},{3,19},{4,20},{5,21},{6,22},{7,23},{8,24},{9,... | collective-permute-start | bytes 2359304 | tf_op jit(solution)/shard_map/ppermute | solution.py:334
  84.7 1.1 copy-done.3
  85.8 18.0 %attend.3 = (bf16[16,96,128]{2,1,0:T(8,128)(2,1)}, bf16[16,192,128]{2,1,0:T(8,128)(2,1)}, f32[16,192,128]{2,1,0:T(8,128)}) custom-call(s32[32]{0:T(128)S(1)} %copy-done.5, s32[1]{0:T(128)} %bitcast.base, bf16[16,192,128]{2,1,0:T(8,128)(2,1)S(1)} %copy-done.3, bf16[16,192,128]{2,1,0:T(8,128)(2,1)S(1)} %all-to-all-done.own, ...), custom_call_target="tpu_custom_call" | custom-call | tf_op jit(solution)/shard_map/attend/pallas_call | solution.py:215
  103.8 4.8 %collective-permute-start.2 = (bf16[16,192,128]{2,1,0:T(8,128)(2,1)}, bf16[16,192,128]{2,1,0:T(8,128)(2,1)S(1)}, u32[]{:S(2)}, u32[]{:S(2)}) collective-permute-start(bf16[16,192,128]{2,1,0:T(8,128)(2,1)} %get-tuple-element.23), channel_id=1, source_target_pairs={{16,0},{17,1},{18,2},{19,3},{20,4},{21,5},{22,6},{23,7},{24,8},{25... | collective-permute-start | bytes 2359304 | tf_op jit(solution)/shard_map/ppermute | solution.py:334
  108.6 7.9 %all-to-all-start.3 = ((bf16[16,96,128]{2,1,0:T(8,128)(2,1)}), bf16[16,96,128]{2,1,0:T(8,128)(2,1)S(1)}, u32[]{:S(2)}, u32[]{:S(2)}) async-start(bf16[16,96,128]{2,1,0:T(8,128)(2,1)} %get-tuple-element.25), calls=%async_computation.3 | async-start | bytes 786432 | tf_op jit(solution)/shard_map/all_to_all | solution.py:329
  116.5 18.5 %attend.2 = (bf16[16,96,128]{2,1,0:T(8,128)(2,1)}, bf16[16,192,128]{2,1,0:T(8,128)(2,1)S(1)}, f32[16,192,128]{2,1,0:T(8,128)}) custom-call(s32[32]{0:T(128)S(1)} %copy-done.5, s32[1]{0:T(128)} %bitcast.base, bf16[16,192,128]{2,1,0:T(8,128)(2,1)} %collective-permute-done.halo, bf16[16,192,128]{2,1,0:T(8,128)(2,1)} %slice.4.own, ...), custom_call_target="tpu_custom_call" | custom-call | tf_op jit(solution)/shard_map/attend/pallas_call | solution.py:215
  135.0 0.9 copy-done.6
  135.9 1.0 copy-done.4
  136.9 1.1 total.2
  138.0 7.4 %all-to-all-start.4 = ((bf16[16,288,128]{2,1,0:T(8,128)(2,1)}), bf16[16,288,128]{2,1,0:T(8,128)(2,1)S(1)}, u32[]{:S(2)}, u32[]{:S(2)}) async-start(bf16[16,288,128]{2,1,0:T(8,128)(2,1)} %total.2), calls=%async_computation.4 | async-start | bytes 2359296 | tf_op jit(solution)/shard_map/all_to_all | solution.py:329
  145.4 2.2 %collective-permute-start.3 = (bf16[16,192,128]{2,1,0:T(8,128)(2,1)}, bf16[16,192,128]{2,1,0:T(8,128)(2,1)S(1)}, u32[]{:S(2)}, u32[]{:S(2)}) collective-permute-start(bf16[16,192,128]{2,1,0:T(8,128)(2,1)} %copy-done.6), channel_id=1, source_target_pairs={{16,0},{17,1},{18,2},{19,3},{20,4},{21,5},{22,6},{23,7},{24,8},{25... | collective-permute-start | bytes 2359304 | tf_op jit(solution)/shard_map/ppermute | solution.py:334
  147.6 19.0 %collective-permute-done.3.refs_1_ = bf16[16,192,128]{2,1,0:T(8,128)(2,1)S(1)} collective-permute-done((bf16[16,192,128]{2,1,0:T(8,128)(2,1)}, bf16[16,192,128]{2,1,0:T(8,128)(2,1)S(1)}, u32[]{:S(2)}, u32[]{:S(2)}) %collective-permute-start.3) | collective-permute-done | bytes 786464 | tf_op jit(solution)/shard_map/ppermute | solution.py:334
  166.6 1.0 total.3
  167.6 8.4 %all-to-all-done.4.refs_1_.refs_0_ = bf16[16,288,128]{2,1,0:T(8,128)(2,1)S(1)} async-done(((bf16[16,288,128]{2,1,0:T(8,128)(2,1)}), bf16[16,288,128]{2,1,0:T(8,128)(2,1)S(1)}, u32[]{:S(2)}, u32[]{:S(2)}) %all-to-all-start.4) | async-done | bytes 1179680 | tf_op jit(solution)/shard_map/all_to_all | solution.py:329
  176.0 3.7 %all-to-all-start.5 = ((bf16[16,192,128]{2,1,0:T(8,128)(2,1)}), bf16[16,192,128]{2,1,0:T(8,128)(2,1)S(1)}, u32[]{:S(2)}, u32[]{:S(2)}) async-start(bf16[16,192,128]{2,1,0:T(8,128)(2,1)} %total.3), calls=%async_computation.5 | async-start | bytes 1572864 | tf_op jit(solution)/shard_map/all_to_all | solution.py:329
  179.7 1.2 unpack.3
  180.8 0.9 unpack.4
  181.7 20.6 %all-to-all-done.5.refs_0_ = bf16[16,192,128]{2,1,0:T(8,128)(2,1)S(1)} async-done(((bf16[16,192,128]{2,1,0:T(8,128)(2,1)}), bf16[16,192,128]{2,1,0:T(8,128)(2,1)S(1)}, u32[]{:S(2)}, u32[]{:S(2)}) %all-to-all-start.5) | async-done | bytes 786464 | tf_op jit(solution)/shard_map/all_to_all | solution.py:329
  202.3 1.0 unpack.5
  (13 shorter events, 0.0 us)
Async XLA Ops:
  2.9 31.8 %all-to-all-start = ((bf16[16,192,128]{2,1,0:T(8,128)(2,1)}), bf16[16,192,128]{2,1,0:T(8,128)(2,1)S(1)}, u32[]{:S(2)}, u32[]{:S(2)}) async-start(bf16[16,192,128]{2,1,0:T(8,128)(2,1)} %pack.4), calls=%async_computation | async-start | bytes 1572864 | tf_op jit(solution)/shard_map/all_to_all | solution.py:329
  34.7 41.6 %all-to-all-start.1 = ((bf16[16,384,128]{2,1,0:T(8,128)(2,1)}), bf16[16,384,128]{2,1,0:T(8,128)(2,1)S(1)}, u32[]{:S(2)}, u32[]{:S(2)}) async-start(bf16[16,384,128]{2,1,0:T(8,128)(2,1)} %pack.3), calls=%async_computation.1 | async-start | bytes 3145728 | tf_op jit(solution)/shard_map/all_to_all | solution.py:329
  38.3 46.4 %copy-start.5 = (s32[32]{0:T(128)S(1)}, s32[32]{0:T(128)}, u32[]{:S(2)}) copy-start(s32[32]{0:T(128)} %lens.3) | copy-start | bytes 388
  38.3 23.4 %collective-permute-start.1 = (bf16[16,192,128]{2,1,0:T(8,128)(2,1)S(1)}, bf16[16,192,128]{2,1,0:T(8,128)(2,1)S(1)}, u32[]{:S(2)}, u32[]{:S(2)}) collective-permute-start(bf16[16,192,128]{2,1,0:T(8,128)(2,1)S(1)} %all-to-all-done.own), channel_id=1, source_target_pairs={{0,16},{1,17},{2,18},{3,19},{4,20},{5,21},{6,22},{7,23},{8,24},{9,... | collective-permute-start | bytes 2359304 | tf_op jit(solution)/shard_map/ppermute | solution.py:334
  61.8 0.9 copy-start.2
  76.3 32.3 %all-to-all-start.2 = ((bf16[16,192,128]{2,1,0:T(8,128)(2,1)}), bf16[16,192,128]{2,1,0:T(8,128)(2,1)S(1)}, u32[]{:S(2)}, u32[]{:S(2)}) async-start(bf16[16,192,128]{2,1,0:T(8,128)(2,1)} %pack.5), calls=%async_computation.2 | async-start | bytes 1572864 | tf_op jit(solution)/shard_map/all_to_all | solution.py:329
  81.5 27.1 %collective-permute-start = (bf16[16,192,128]{2,1,0:T(8,128)(2,1)}, bf16[16,192,128]{2,1,0:T(8,128)(2,1)}, u32[]{:S(2)}, u32[]{:S(2)}) collective-permute-start(bf16[16,192,128]{2,1,0:T(8,128)(2,1)} %slice.4.own), channel_id=1, source_target_pairs={{0,16},{1,17},{2,18},{3,19},{4,20},{5,21},{6,22},{7,23},{8,24},{9,... | collective-permute-start | bytes 2359304 | tf_op jit(solution)/shard_map/ppermute | solution.py:334
  84.7 1.1 copy-start.3
  103.8 31.3 %collective-permute-start.2 = (bf16[16,192,128]{2,1,0:T(8,128)(2,1)}, bf16[16,192,128]{2,1,0:T(8,128)(2,1)S(1)}, u32[]{:S(2)}, u32[]{:S(2)}) collective-permute-start(bf16[16,192,128]{2,1,0:T(8,128)(2,1)} %get-tuple-element.23), channel_id=1, source_target_pairs={{16,0},{17,1},{18,2},{19,3},{20,4},{21,5},{22,6},{23,7},{24,8},{25... | collective-permute-start | bytes 2359304 | tf_op jit(solution)/shard_map/ppermute | solution.py:334
  108.6 27.3 %copy-start.1 = (f32[16,192,128]{2,1,0:T(8,128)S(1)}, f32[16,192,128]{2,1,0:T(8,128)}, u32[]{:S(2)}) copy-start(f32[16,192,128]{2,1,0:T(8,128)} %get-tuple-element.22.refs_1_) | copy-start | bytes 4718596
  108.6 29.4 %all-to-all-start.3 = ((bf16[16,96,128]{2,1,0:T(8,128)(2,1)}), bf16[16,96,128]{2,1,0:T(8,128)(2,1)S(1)}, u32[]{:S(2)}, u32[]{:S(2)}) async-start(bf16[16,96,128]{2,1,0:T(8,128)(2,1)} %get-tuple-element.25), calls=%async_computation.3 | async-start | bytes 786432 | tf_op jit(solution)/shard_map/all_to_all | solution.py:329
  135.0 0.9 copy-start.6
  135.9 1.0 copy-start.4
  138.0 28.6 %copy-start = (f32[16,192,128]{2,1,0:T(8,128)S(1)}, f32[16,192,128]{2,1,0:T(8,128)}, u32[]{:S(2)}) copy-start(f32[16,192,128]{2,1,0:T(8,128)} %get-tuple-element.28.refs_0_) | copy-start | bytes 4718596
  138.0 37.9 %all-to-all-start.4 = ((bf16[16,288,128]{2,1,0:T(8,128)(2,1)}), bf16[16,288,128]{2,1,0:T(8,128)(2,1)S(1)}, u32[]{:S(2)}, u32[]{:S(2)}) async-start(bf16[16,288,128]{2,1,0:T(8,128)(2,1)} %total.2), calls=%async_computation.4 | async-start | bytes 2359296 | tf_op jit(solution)/shard_map/all_to_all | solution.py:329
  145.4 21.2 %collective-permute-start.3 = (bf16[16,192,128]{2,1,0:T(8,128)(2,1)}, bf16[16,192,128]{2,1,0:T(8,128)(2,1)S(1)}, u32[]{:S(2)}, u32[]{:S(2)}) collective-permute-start(bf16[16,192,128]{2,1,0:T(8,128)(2,1)} %copy-done.6), channel_id=1, source_target_pairs={{16,0},{17,1},{18,2},{19,3},{20,4},{21,5},{22,6},{23,7},{24,8},{25... | collective-permute-start | bytes 2359304 | tf_op jit(solution)/shard_map/ppermute | solution.py:334
  176.0 26.4 %all-to-all-start.5 = ((bf16[16,192,128]{2,1,0:T(8,128)(2,1)}), bf16[16,192,128]{2,1,0:T(8,128)(2,1)S(1)}, u32[]{:S(2)}, u32[]{:S(2)}) async-start(bf16[16,192,128]{2,1,0:T(8,128)(2,1)} %total.3), calls=%async_computation.5 | async-start | bytes 1572864 | tf_op jit(solution)/shard_map/all_to_all | solution.py:329
